TPU v7x, 32 devices: a whole 2x2x4 slice. The times are simulated.
32 devices in a mesh: groups: 2 (over y), row: 16 (over z, x, core).
Axes of the slice: x: 2, y: 2, z: 4, core: 2. Of those that a mesh axis runs over, the one named last changes fastest.
Arguments:
- b3_store: bfloat16 [384, 5, 68, 576], P(('groups', 'row')), parts along dimension 0, may hold values from -1.1953125 to 1.1953125
- block_shift: int32 [24, 5], P('groups'), parts along dimension 0, may hold values from 0 to 15, as said below
- green: bfloat16 [2, 2, 384, 5, 576], P(None, None, ('groups', 'row')), parts along dimension 2, may hold values from -0.4 to 1.4, as said below
- block_mask: int32 [384, 5], P(('groups', 'row')), parts along dimension 0, may hold values 0 or 1
Outputs:
- chi_blocks: float32 [2, 384, 5, 4624], P(None, ('groups', 'row')), parts along dimension 1
There are 2 independent parts, one for each index of `groups`. A program takes and returns all parts, laid end to end along the dimension named above; each array names one. Nothing has to cross between parts.
Inputs may be any that keep to these rules, and one draw needn't show every extreme that they name: `block_shift`: no value is taken by more than 4 entries, and some value by exactly 4. green[k, t, m, s] is the transpose of the block green[k, t, (m + s - 2) mod 192, 4 - s].
All inputs are finite; a program needn't handle non-finite values. No bound on the sum of `block_mask` on one device may be relied on, other than what follows from the above.
Results may differ from a plain program's by a relative error of at most 0.0012.
Values may be sent and summed in bfloat16 or wider, within the bound.
No kernel may reach another device: no remote copies, remote signals or barrier semaphores. Data moves between devices by JAX's collectives and lax.ppermute only.
A program may use at most 192 MiB of HBM per device.

v0:
```python
import jax
import jax.numpy as jnp
from jax import lax
from jax.sharding import PartitionSpec as P

BO = 24
HALF = 2
NTAU = 2
NN = 5
NW = 9


def padded(shard, sides, width):
    for axis, dim in sides:
        count, length = (lax.axis_size(axis), shard.shape[dim])
        up = [(i, (i + 1) % count) for i in range(count)]
        down = [(j, i) for i, j in up]
        last = lax.slice_in_dim(shard, length - width, length, axis=dim)
        leading = lax.slice_in_dim(shard, 0, width, axis=dim)
        before = lax.ppermute(last, axis, up)
        after = lax.ppermute(leading, axis, down)
        shard = jnp.concatenate([before, shard, after], axis=dim)
    return shard


def shards(b3_store, block_shift, green, block_mask):
    devices = lax.axis_size("row")
    myself = lax.axis_index("row")
    mol_dev = b3_store.shape[0]
    aux_count = b3_store.shape[2]
    pair_size = b3_store.shape[3]
    block_count = mol_dev * NN
    capacity = (block_count + devices - 1) // devices
    shifts = block_shift.reshape(block_count)
    position = jnp.arange(block_count, dtype=jnp.int32)
    same_shift = (shifts[:, None] == shifts[None, :]) & (position[None, :] < position[:, None])
    slot_rank = jnp.sum(same_shift.astype(jnp.int32), axis=1)
    target = (myself - shifts) % devices
    outgoing = jnp.zeros((devices, capacity, aux_count, pair_size), jnp.bfloat16)
    outgoing = outgoing.at[target, slot_rank].set(
        b3_store.reshape(block_count, aux_count, pair_size)
    )
    incoming = lax.all_to_all(outgoing, "row", split_axis=0, concat_axis=0, tiled=True)
    anchor = (myself + shifts) % devices
    blocks = incoming[anchor, slot_rank].reshape(mol_dev, NN, aux_count, pair_size)
    blocks = blocks * block_mask.astype(jnp.bfloat16)[:, :, None, None]
    virtual = padded(green[1], (("row", 1),), HALF)
    pieces = []
    for offset in range(NN):
        window_rows = virtual[:, offset : offset + mol_dev].reshape(NTAU, mol_dev, NN, BO, BO)
        pieces.append(
            jnp.pad(window_rows, ((0, 0), (0, 0), (offset, NW - NN - offset), (0, 0), (0, 0)))
        )
    window = jnp.stack(pieces, axis=2)
    window = jnp.transpose(window, (0, 1, 2, 4, 3, 5)).reshape(NTAU, mol_dev, NN, BO, NW * BO)
    occupied = green[0].reshape(NTAU, mol_dev, NN, BO, BO)
    partners = padded(blocks, (("row", 0),), HALF)
    reach_slots = NN

    def molecule_chi(local_index):
        own_blocks = lax.dynamic_index_in_dim(blocks, local_index, 0, keepdims=False)
        own_blocks = own_blocks.reshape(NN, aux_count * BO, BO)
        near_blocks = lax.dynamic_slice_in_dim(partners, local_index, reach_slots, 0)
        near_blocks = near_blocks.reshape(reach_slots, NN, aux_count, BO, BO)
        results = []
        for time_point in range(NTAU):
            green_window = lax.dynamic_index_in_dim(
                window[time_point], local_index, 0, keepdims=False
            )
            spread = jnp.einsum(
                "sxi,siy->xy", own_blocks, green_window, preferred_element_type=jnp.float32
            )
            spread = spread.astype(jnp.bfloat16).reshape(aux_count, BO, NW * BO)
            occupied_rows = lax.dynamic_index_in_dim(
                occupied[time_point], local_index, 0, keepdims=False
            )
            folded = jnp.einsum(
                "pmy,wml->pwly", spread, occupied_rows, preferred_element_type=jnp.float32
            )
            folded = folded.astype(jnp.bfloat16).reshape(aux_count, reach_slots, BO, NW, BO)
            chi_list = []
            for offset in range(reach_slots):
                window_part = folded[:, offset, :, offset : offset + NN, :]
                chi_list.append(
                    jnp.einsum(
                        "pluj,uqlj->pq",
                        window_part,
                        near_blocks[offset],
                        preferred_element_type=jnp.float32,
                    ).reshape(aux_count * aux_count)
                )
            results.append(jnp.stack(chi_list))
        return jnp.stack(results)

    def run_group(group_index):
        return jax.vmap(molecule_chi)(group_index * 4 + jnp.arange(4, dtype=jnp.int32))

    stacked = lax.map(run_group, jnp.arange(mol_dev // 4, dtype=jnp.int32))
    stacked = stacked.reshape(mol_dev, NTAU, reach_slots, aux_count * aux_count)
    computed = jnp.transpose(stacked, (1, 0, 2, 3))
    return computed


def solution(mesh):
    in_specs = (
        P(("groups", "row"), None, None, None),
        P("groups", None),
        P(None, None, ("groups", "row"), None, None),
        P(("groups", "row"), None),
    )
    out_specs = P(None, ("groups", "row"), None, None)
    return jax.shard_map(shards, mesh=mesh, in_specs=in_specs, out_specs=out_specs, check_vma=False)
```

profile of v0, /device:TPU:0, one launch (start us, length us, event | category | flops | bytes accessed | tf_op | source)
XLA Modules:
  0.0 916.8 jit_solution(12173442494339815697)
XLA Ops:
  5.1 19.9 %scatter_fusion = bf16[16,4,68,576]{3,2,1,0:T(8,128)(2,1)} fusion(bf16[16,4,68,576]{3,2,1,0:T(8,128)(2,1)} %broadcast_in_dim.16, s32[60]{0:T(128)S(1)} %get-tuple-element.138, bf16[60,68,576]{2,1,0:T(8,128)(2,1)} %bitcast.351), kind=kCustom, calls=%fused_computation.6 | custom fusion | bytes 14100960 | tf_op jit(solution)/shard_map/scatter | solution.py:40
  47.4 94.2 %all-to-all-done = bf16[16,4,68,576]{3,1,2,0:T(4,128)(2,1)} async-done(((bf16[16,4,68,576]{3,1,2,0:T(4,128)(2,1)}), bf16[16,4,68,576]{3,1,2,0:T(4,128)(2,1)}, u32[]{:S(2)}, u32[]{:S(2)}) %all-to-all-start) | async-done | bytes 5013536 | tf_op jit(solution)/shard_map/all_to_all | solution.py:43
  161.8 23.2 %collective-permute-start.3 = (bf16[2,5,68,576]{3,0,2,1:T(2,128)(2,1)}, bf16[2,5,68,576]{3,0,2,1:T(2,128)(2,1)}, u32[]{:S(2)}, u32[]{:S(2)}) collective-permute-start(bf16[2,5,68,576]{3,0,2,1:T(2,128)(2,1)} %copy.185), channel_id=1, source_target_pairs={{1,0},{2,1},{3,2},{4,3},{5,4},{6,5},{7,6},{8,7},{9,8},{10,9},{11,1... | collective-permute-start | bytes 2350088 | tf_op jit(solution)/shard_map/ppermute | solution.py:21
  216.0 700.5 %while.13 = (s32[]{:T(128)}, f32[3,4,2,5,4624]{4,2,3,1,0:T(2,128)}, bf16[2,12,5,24,24]{4,3,2,1,0:T(8,128)(2,1)}, s32[3]{0:T(128)}, bf16[12,5,68,576]{3,2,1,0:T(8...) while((s32[]{:T(128)}, f32[3,4,2,5,4624]{4,2,3,1,0:T(2,128)}, ...), condition=%wide.region_3.4_spmd, body=%wide.region_2.3_spmd.sunk | while | flops 2436121088 | bytes 276545376 | solution.py:98
  272.9 30.7 %copy.357 = bf16[4,68,5,24,216]{1,4,3,2,0:T(8,128)(2,1)} copy(bf16[4,68,5,24,216]{4,3,1,2,0:T(8,128)(2,1)} %convert_bitcast_fusion.5) | data formatting | bytes 28200960 | tf_op jit(solution)/shard_map/while/body/eval_jaxpr/vmap()/convert_element_type | solution.py:80
  303.6 10.7 %fusion.84 = (bf16[4,68,1,24,5,24]{1,5,4,3,2,0:T(8,128)(2,1)}, bf16[4,68,1,24,5,24]{1,5,4,3,2,0:T(8,128)(2,1)}, bf16[4,68,1,24,5,24]{1,5,4,3,2,0:T(8,128)(2,1)},...) fusion(bf16[4,68,5,24,9,24]{1,5,4,3,2,0:T(8,128)(2,1)} %bitcast.342), kind=kLoop, calls=%fused_computation.114.clone.1 | loop fusion | bytes 15667200 | tf_op jit(solution)/shard_map/while/body/eval_jaxpr/vmap()/slice | solution.py:83
  314.5 13.2 %while.14 = (s32[]{:T(128)}, bf16[16,5,68,576]{3,2,1,0:T(8,128)(2,1)}, s32[4,4]{1,0:T(4,128)S(1)}, bf16[4,5,5,68,576]{4,3,2,1,0:T(8,128)(2,1)}, s32[]{:T(128)}) while((s32[]{:T(128)}, bf16[16,5,68,576]{3,2,1,0:T(8,128)(2,1)}, s32[4,4]{1,0:T(4,128)S(1)}, bf16[4,5,5,68,576]{4,3,2,1,0:T(8,128)(2,1)}, s32[]{:T(128)}) %tuple.74), condition=%wide.while_cond, body=%wide.while_body.sunk | while | flops 2 | bytes 4608613 | solution.py:63
  327.7 17.6 %copy.353 = bf16[4,5,5,68,576]{3,4,2,1,0:T(8,128)(2,1)} copy(bf16[4,5,5,68,576]{4,3,2,1,0:T(8,128)(2,1)} %get-tuple-element.234) | data formatting | bytes 15667200 | tf_op jit(solution)/shard_map/while/body/eval_jaxpr/vmap()/gather | solution.py:63
  345.3 9.5 %fusion.77 = (bf16[4,1,5,68,24,24]{3,5,4,2,1,0:T(8,128)(2,1)S(1)}, bf16[4,1,5,68,24,24]{3,5,4,2,1,0:T(8,128)(2,1)}, bf16[4,1,5,68,24,24]{3,5,4,2,1,0:T(8,128)(2,...) fusion(bf16[4,5,5,68,24,24]{3,5,4,2,1,0:T(8,128)(2,1)} %bitcast.344), kind=kLoop, calls=%fused_computation.116.clone.1 | loop fusion | bytes 15667200 | tf_op jit(solution)/shard_map/while/body/eval_jaxpr/vmap()/slice | solution.py:88
  401.4 30.7 %copy.355 = bf16[4,68,5,24,216]{1,4,3,2,0:T(8,128)(2,1)} copy(bf16[4,68,5,24,216]{4,3,1,2,0:T(8,128)(2,1)} %convert_bitcast_fusion.4) | data formatting | bytes 28200960 | tf_op jit(solution)/shard_map/while/body/eval_jaxpr/vmap()/convert_element_type | solution.py:80
  432.1 10.4 %fusion.78 = (bf16[4,68,1,24,5,24]{1,5,4,3,2,0:T(8,128)(2,1)}, bf16[4,68,1,24,5,24]{1,5,4,3,2,0:T(8,128)(2,1)}, bf16[4,68,1,24,5,24]{1,5,4,3,2,0:T(8,128)(2,1)},...) fusion(bf16[4,68,5,24,9,24]{1,5,4,3,2,0:T(8,128)(2,1)} %bitcast.343), kind=kLoop, calls=%fused_computation.115.clone.1 | loop fusion | bytes 15667200 | tf_op jit(solution)/shard_map/while/body/eval_jaxpr/vmap()/slice | solution.py:83
  500.1 30.7 %copy.357 = bf16[4,68,5,24,216]{1,4,3,2,0:T(8,128)(2,1)} copy(bf16[4,68,5,24,216]{4,3,1,2,0:T(8,128)(2,1)} %convert_bitcast_fusion.5) | data formatting | bytes 28200960 | tf_op jit(solution)/shard_map/while/body/eval_jaxpr/vmap()/convert_element_type | solution.py:80
  530.8 10.7 %fusion.84 = (bf16[4,68,1,24,5,24]{1,5,4,3,2,0:T(8,128)(2,1)}, bf16[4,68,1,24,5,24]{1,5,4,3,2,0:T(8,128)(2,1)}, bf16[4,68,1,24,5,24]{1,5,4,3,2,0:T(8,128)(2,1)},...) fusion(bf16[4,68,5,24,9,24]{1,5,4,3,2,0:T(8,128)(2,1)} %bitcast.342), kind=kLoop, calls=%fused_computation.114.clone.1 | loop fusion | bytes 15667200 | tf_op jit(solution)/shard_map/while/body/eval_jaxpr/vmap()/slice | solution.py:83
  541.7 13.2 %while.14 = (s32[]{:T(128)}, bf16[16,5,68,576]{3,2,1,0:T(8,128)(2,1)}, s32[4,4]{1,0:T(4,128)S(1)}, bf16[4,5,5,68,576]{4,3,2,1,0:T(8,128)(2,1)}, s32[]{:T(128)}) while((s32[]{:T(128)}, bf16[16,5,68,576]{3,2,1,0:T(8,128)(2,1)}, s32[4,4]{1,0:T(4,128)S(1)}, bf16[4,5,5,68,576]{4,3,2,1,0:T(8,128)(2,1)}, s32[]{:T(128)}) %tuple.74), condition=%wide.while_cond, body=%wide.while_body.sunk | while | flops 2 | bytes 4608613 | solution.py:63
  554.9 17.6 %copy.353 = bf16[4,5,5,68,576]{3,4,2,1,0:T(8,128)(2,1)} copy(bf16[4,5,5,68,576]{4,3,2,1,0:T(8,128)(2,1)} %get-tuple-element.234) | data formatting | bytes 15667200 | tf_op jit(solution)/shard_map/while/body/eval_jaxpr/vmap()/gather | solution.py:63
  572.5 9.5 %fusion.77 = (bf16[4,1,5,68,24,24]{3,5,4,2,1,0:T(8,128)(2,1)S(1)}, bf16[4,1,5,68,24,24]{3,5,4,2,1,0:T(8,128)(2,1)}, bf16[4,1,5,68,24,24]{3,5,4,2,1,0:T(8,128)(2,...) fusion(bf16[4,5,5,68,24,24]{3,5,4,2,1,0:T(8,128)(2,1)} %bitcast.344), kind=kLoop, calls=%fused_computation.116.clone.1 | loop fusion | bytes 15667200 | tf_op jit(solution)/shard_map/while/body/eval_jaxpr/vmap()/slice | solution.py:88
  628.6 30.7 %copy.355 = bf16[4,68,5,24,216]{1,4,3,2,0:T(8,128)(2,1)} copy(bf16[4,68,5,24,216]{4,3,1,2,0:T(8,128)(2,1)} %convert_bitcast_fusion.4) | data formatting | bytes 28200960 | tf_op jit(solution)/shard_map/while/body/eval_jaxpr/vmap()/convert_element_type | solution.py:80
  659.3 10.4 %fusion.78 = (bf16[4,68,1,24,5,24]{1,5,4,3,2,0:T(8,128)(2,1)}, bf16[4,68,1,24,5,24]{1,5,4,3,2,0:T(8,128)(2,1)}, bf16[4,68,1,24,5,24]{1,5,4,3,2,0:T(8,128)(2,1)},...) fusion(bf16[4,68,5,24,9,24]{1,5,4,3,2,0:T(8,128)(2,1)} %bitcast.343), kind=kLoop, calls=%fused_computation.115.clone.1 | loop fusion | bytes 15667200 | tf_op jit(solution)/shard_map/while/body/eval_jaxpr/vmap()/slice | solution.py:83
  727.3 30.7 %copy.357 = bf16[4,68,5,24,216]{1,4,3,2,0:T(8,128)(2,1)} copy(bf16[4,68,5,24,216]{4,3,1,2,0:T(8,128)(2,1)} %convert_bitcast_fusion.5) | data formatting | bytes 28200960 | tf_op jit(solution)/shard_map/while/body/eval_jaxpr/vmap()/convert_element_type | solution.py:80
  758.0 10.7 %fusion.84 = (bf16[4,68,1,24,5,24]{1,5,4,3,2,0:T(8,128)(2,1)}, bf16[4,68,1,24,5,24]{1,5,4,3,2,0:T(8,128)(2,1)}, bf16[4,68,1,24,5,24]{1,5,4,3,2,0:T(8,128)(2,1)},...) fusion(bf16[4,68,5,24,9,24]{1,5,4,3,2,0:T(8,128)(2,1)} %bitcast.342), kind=kLoop, calls=%fused_computation.114.clone.1 | loop fusion | bytes 15667200 | tf_op jit(solution)/shard_map/while/body/eval_jaxpr/vmap()/slice | solution.py:83
  768.9 13.2 %while.14 = (s32[]{:T(128)}, bf16[16,5,68,576]{3,2,1,0:T(8,128)(2,1)}, s32[4,4]{1,0:T(4,128)S(1)}, bf16[4,5,5,68,576]{4,3,2,1,0:T(8,128)(2,1)}, s32[]{:T(128)}) while((s32[]{:T(128)}, bf16[16,5,68,576]{3,2,1,0:T(8,128)(2,1)}, s32[4,4]{1,0:T(4,128)S(1)}, bf16[4,5,5,68,576]{4,3,2,1,0:T(8,128)(2,1)}, s32[]{:T(128)}) %tuple.74), condition=%wide.while_cond, body=%wide.while_body.sunk | while | flops 2 | bytes 4608613 | solution.py:63
  782.1 17.6 %copy.353 = bf16[4,5,5,68,576]{3,4,2,1,0:T(8,128)(2,1)} copy(bf16[4,5,5,68,576]{4,3,2,1,0:T(8,128)(2,1)} %get-tuple-element.234) | data formatting | bytes 15667200 | tf_op jit(solution)/shard_map/while/body/eval_jaxpr/vmap()/gather | solution.py:63
  855.8 30.7 %copy.355 = bf16[4,68,5,24,216]{1,4,3,2,0:T(8,128)(2,1)} copy(bf16[4,68,5,24,216]{4,3,1,2,0:T(8,128)(2,1)} %convert_bitcast_fusion.4) | data formatting | bytes 28200960 | tf_op jit(solution)/shard_map/while/body/eval_jaxpr/vmap()/convert_element_type | solution.py:80
  886.5 10.4 %fusion.78 = (bf16[4,68,1,24,5,24]{1,5,4,3,2,0:T(8,128)(2,1)}, bf16[4,68,1,24,5,24]{1,5,4,3,2,0:T(8,128)(2,1)}, bf16[4,68,1,24,5,24]{1,5,4,3,2,0:T(8,128)(2,1)},...) fusion(bf16[4,68,5,24,9,24]{1,5,4,3,2,0:T(8,128)(2,1)} %bitcast.343), kind=kLoop, calls=%fused_computation.115.clone.1 | loop fusion | bytes 15667200 | tf_op jit(solution)/shard_map/while/body/eval_jaxpr/vmap()/slice | solution.py:83
  (307 shorter events, 438.3 us)
Async XLA Ops:
  32.2 7.4 copy-start.13
  32.2 109.4 %all-to-all-start = ((bf16[16,4,68,576]{3,1,2,0:T(4,128)(2,1)}), bf16[16,4,68,576]{3,1,2,0:T(4,128)(2,1)}, u32[]{:S(2)}, u32[]{:S(2)}) async-start(bf16[16,4,68,576]{3,1,2,0:T(4,128)(2,1)} %copy.175), calls=%async_computation | async-start | bytes 11141120 | tf_op jit(solution)/shard_map/all_to_all | solution.py:43
  39.7 5.9 copy-start.14
  40.0 144.9 %collective-permute-start = (bf16[2,2,5,576]{3,0,2,1:T(2,128)(2,1)S(1)}, bf16[2,2,5,576]{3,0,2,1:T(2,128)(2,1)S(1)}, u32[]{:S(2)}, u32[]{:S(2)}) collective-permute-start(bf16[2,2,5,576]{3,0,2,1:T(2,128)(2,1)S(1)} %get-tuple-element.134), channel_id=1, source_target_pairs={{0,1},{1,2},{2,3},{3,4},{4,5},{5,6},{6,7},{7,8},{8,9},{9,10},{10,1... | collective-permute-start | bytes 69128 | tf_op jit(solution)/shard_map/ppermute | solution.py:20
  40.4 144.5 %collective-permute-start.1 = (bf16[2,2,5,576]{3,0,2,1:T(2,128)(2,1)S(1)}, bf16[2,2,5,576]{3,0,2,1:T(2,128)(2,1)S(1)}, u32[]{:S(2)}, u32[]{:S(2)}) collective-permute-start(bf16[2,2,5,576]{3,0,2,1:T(2,128)(2,1)S(1)} %get-tuple-element.133), channel_id=1, source_target_pairs={{1,0},{2,1},{3,2},{4,3},{5,4},{6,5},{7,6},{8,7},{9,8},{10,9},{11,1... | collective-permute-start | bytes 69128 | tf_op jit(solution)/shard_map/ppermute | solution.py:21
  157.0 4.7 copy-start
  159.4 45.2 %collective-permute-start.2 = (bf16[2,5,68,576]{3,0,2,1:T(2,128)(2,1)}, bf16[2,5,68,576]{3,0,2,1:T(2,128)(2,1)}, u32[]{:S(2)}, u32[]{:S(2)}) collective-permute-start(bf16[2,5,68,576]{3,0,2,1:T(2,128)(2,1)} %copy.184), channel_id=1, source_target_pairs={{0,1},{1,2},{2,3},{3,4},{4,5},{5,6},{6,7},{7,8},{8,9},{9,10},{10,1... | collective-permute-start | bytes 2350088 | tf_op jit(solution)/shard_map/ppermute | solution.py:20
  161.8 44.1 %collective-permute-start.3 = (bf16[2,5,68,576]{3,0,2,1:T(2,128)(2,1)}, bf16[2,5,68,576]{3,0,2,1:T(2,128)(2,1)}, u32[]{:S(2)}, u32[]{:S(2)}) collective-permute-start(bf16[2,5,68,576]{3,0,2,1:T(2,128)(2,1)} %copy.185), channel_id=1, source_target_pairs={{1,0},{2,1},{3,2},{4,3},{5,4},{6,5},{7,6},{8,7},{9,8},{10,9},{11,1... | collective-permute-start | bytes 2350088 | tf_op jit(solution)/shard_map/ppermute | solution.py:21
  234.8 14.0 %copy-start.7 = (bf16[2,12,5,24,216]{4,3,2,1,0:T(8,128)(2,1)}, bf16[2,12,5,24,216]{4,3,2,1,0:T(8,128)(2,1)S(1)}, u32[]{:S(2)}) copy-start(bf16[2,12,5,24,216]{4,3,2,1,0:T(8,128)(2,1)S(1)} %get-tuple-element.302) | copy-start | bytes 3732484 | tf_op jit(solution)/shard_map/while
  345.3 11.1 %copy-start.6 = (bf16[4,68,1,24,5,24]{1,5,4,3,2,0:T(8,128)(2,1)S(1)}, bf16[4,68,1,24,5,24]{1,5,4,3,2,0:T(8,128)(2,1)}, u32[]{:S(2)}) copy-start(bf16[4,68,1,24,5,24]{1,5,4,3,2,0:T(8,128)(2,1)} %get-tuple-element.250) | copy-start | bytes 4700164 | tf_op jit(solution)/shard_map/while
  354.8 19.5 %copy-start.1 = (bf16[4,1,5,68,24,24]{3,5,4,2,1,0:T(8,128)(2,1)}, bf16[4,1,5,68,24,24]{3,5,4,2,1,0:T(8,128)(2,1)S(1)}, u32[]{:S(2)}) copy-start(bf16[4,1,5,68,24,24]{3,5,4,2,1,0:T(8,128)(2,1)S(1)} %get-tuple-element.246) | copy-start | bytes 4700164 | tf_op jit(solution)/shard_map/while
  432.1 10.4 %copy-start.5 = (bf16[4,1,5,68,24,24]{3,5,4,2,1,0:T(8,128)(2,1)S(1)}, bf16[4,1,5,68,24,24]{3,5,4,2,1,0:T(8,128)(2,1)}, u32[]{:S(2)}) copy-start(bf16[4,1,5,68,24,24]{3,5,4,2,1,0:T(8,128)(2,1)} %copy-done.4) | copy-start | bytes 4700164 | tf_op jit(solution)/shard_map/while
  443.7 4.1 copy-start.3
  450.9 4.9 copy-start.2
  462.0 13.9 %copy-start.7 = (bf16[2,12,5,24,216]{4,3,2,1,0:T(8,128)(2,1)}, bf16[2,12,5,24,216]{4,3,2,1,0:T(8,128)(2,1)S(1)}, u32[]{:S(2)}) copy-start(bf16[2,12,5,24,216]{4,3,2,1,0:T(8,128)(2,1)S(1)} %get-tuple-element.302) | copy-start | bytes 3732484 | tf_op jit(solution)/shard_map/while
  572.5 11.1 %copy-start.6 = (bf16[4,68,1,24,5,24]{1,5,4,3,2,0:T(8,128)(2,1)S(1)}, bf16[4,68,1,24,5,24]{1,5,4,3,2,0:T(8,128)(2,1)}, u32[]{:S(2)}) copy-start(bf16[4,68,1,24,5,24]{1,5,4,3,2,0:T(8,128)(2,1)} %get-tuple-element.250) | copy-start | bytes 4700164 | tf_op jit(solution)/shard_map/while
  582.0 19.5 %copy-start.1 = (bf16[4,1,5,68,24,24]{3,5,4,2,1,0:T(8,128)(2,1)}, bf16[4,1,5,68,24,24]{3,5,4,2,1,0:T(8,128)(2,1)S(1)}, u32[]{:S(2)}) copy-start(bf16[4,1,5,68,24,24]{3,5,4,2,1,0:T(8,128)(2,1)S(1)} %get-tuple-element.246) | copy-start | bytes 4700164 | tf_op jit(solution)/shard_map/while
  659.3 10.4 %copy-start.5 = (bf16[4,1,5,68,24,24]{3,5,4,2,1,0:T(8,128)(2,1)S(1)}, bf16[4,1,5,68,24,24]{3,5,4,2,1,0:T(8,128)(2,1)}, u32[]{:S(2)}) copy-start(bf16[4,1,5,68,24,24]{3,5,4,2,1,0:T(8,128)(2,1)} %copy-done.4) | copy-start | bytes 4700164 | tf_op jit(solution)/shard_map/while
  678.1 4.9 copy-start.2
  689.2 13.9 %copy-start.7 = (bf16[2,12,5,24,216]{4,3,2,1,0:T(8,128)(2,1)}, bf16[2,12,5,24,216]{4,3,2,1,0:T(8,128)(2,1)S(1)}, u32[]{:S(2)}) copy-start(bf16[2,12,5,24,216]{4,3,2,1,0:T(8,128)(2,1)S(1)} %get-tuple-element.302) | copy-start | bytes 3732484 | tf_op jit(solution)/shard_map/while
  799.7 11.1 %copy-start.6 = (bf16[4,68,1,24,5,24]{1,5,4,3,2,0:T(8,128)(2,1)S(1)}, bf16[4,68,1,24,5,24]{1,5,4,3,2,0:T(8,128)(2,1)}, u32[]{:S(2)}) copy-start(bf16[4,68,1,24,5,24]{1,5,4,3,2,0:T(8,128)(2,1)} %get-tuple-element.250) | copy-start | bytes 4700164 | tf_op jit(solution)/shard_map/while
  809.2 19.5 %copy-start.1 = (bf16[4,1,5,68,24,24]{3,5,4,2,1,0:T(8,128)(2,1)}, bf16[4,1,5,68,24,24]{3,5,4,2,1,0:T(8,128)(2,1)S(1)}, u32[]{:S(2)}) copy-start(bf16[4,1,5,68,24,24]{3,5,4,2,1,0:T(8,128)(2,1)S(1)} %get-tuple-element.246) | copy-start | bytes 4700164 | tf_op jit(solution)/shard_map/while
  886.5 10.4 %copy-start.5 = (bf16[4,1,5,68,24,24]{3,5,4,2,1,0:T(8,128)(2,1)S(1)}, bf16[4,1,5,68,24,24]{3,5,4,2,1,0:T(8,128)(2,1)}, u32[]{:S(2)}) copy-start(bf16[4,1,5,68,24,24]{3,5,4,2,1,0:T(8,128)(2,1)} %copy-done.4) | copy-start | bytes 4700164 | tf_op jit(solution)/shard_map/while
  905.3 4.9 copy-start.2
  (16 other events, 34.9 us)
where the time goes:
time: 933 us; the launch traced here: 917 us
  local copies, waits for them, and re-layouts  554 us (59%)
  matrix products  194 us (21%)
  waiting for transfers between devices  94.2 us (10%)
  starting transfers between devices  35.9 us (4%)
  loops' own time  21.3 us (2%)
  other arithmetic  17.5 us (2%)
    convert_element_type x6, local copies, waits for them, and re-layouts, molecule_chi(): folded.astype(jnp.bfloat16).reshape(aux_count, reach_slots, BO, NW, BO)  184 us
    dot_general x30, matrix products, molecule_chi(): jnp.einsum('pluj,uqlj->pq', window_part, near_blocks[offset], preferred_e...  98.7 us
    all_to_all x1, waiting for transfers between devices, shards(): lax.all_to_all(outgoing, 'row', split_axis=0, concat_axis=0, tiled=True)  94.2 us
    slice x6, local copies, waits for them, and re-layouts, molecule_chi(): window_part = folded[:, offset, :, offset:offset + NN, :]  63.3 us
    gather x3, local copies, waits for them, and re-layouts, molecule_chi(): lax.dynamic_slice_in_dim(partners, local_index, reach_slots, 0)  52.8 us
    dot_general x6, matrix products, molecule_chi(): jnp.einsum('sxi,siy->xy', own_blocks, green_window, preferred_element_typ...  47.5 us
    dot_general x6, matrix products, molecule_chi(): jnp.einsum('pmy,wml->pwly', spread, occupied_rows, preferred_element_type...  47.4 us
    gather x24, local copies, waits for them, and re-layouts  39.6 us
  transfers between devices with their start and end apart: 5, of which 1 were waited for; matrix products, arithmetic and copies ran while one was open for 4% of the time, Pallas kernels for 0%

commit v1 on v0

v1 whole, which is shorter than its diff:
```python
import functools

import jax
import jax.numpy as jnp
import numpy as np
from jax import lax
from jax.experimental import pallas as pl
from jax.experimental.pallas import tpu as pltpu
from jax.sharding import PartitionSpec as P

BO = 24
HALF = 2
NTAU = 2
NN = 5
NW = 9
LANE = 128
KEPT = 3
BF = jnp.bfloat16
F32 = jnp.float32
VMEM_LIMIT = 56 * 1024 * 1024


def call(body, name, grid, in_specs, out_specs, out_shape, scratch=(), prefetch=0):
    return pl.pallas_call(
        body,
        grid_spec=pltpu.PrefetchScalarGridSpec(
            num_scalar_prefetch=prefetch,
            grid=grid,
            in_specs=in_specs,
            out_specs=out_specs,
            scratch_shapes=list(scratch),
        ),
        out_shape=out_shape,
        name=name,
        compiler_params=pltpu.CompilerParams(vmem_limit_bytes=VMEM_LIMIT),
    )


def chunk_groups(aux):
    full = aux // 16
    last = [full] if aux % 16 else []
    return [list(range(full - 1)) + last, [full - 1]]


def piece_rows(groups, aux):
    return [min(16, aux - 16 * g) for g in groups]


def piece_starts(groups, aux, halves):
    starts, row = [], 0
    for height in piece_rows(groups, aux):
        starts.append(row)
        row += height * halves
    return starts, row


def pack_blocks(store, target, rank, devices, capacity, groups):
    count, aux, size = store.shape
    pair = 2 if capacity > 1 else 1
    halves = (capacity + pair - 1) // pair
    heights = piece_rows(groups, aux)
    starts, total = piece_starts(groups, aux, halves)
    steps = 4
    batch = count // steps

    def body(target_ref, rank_ref, *refs):
        out_ref = refs[-1]
        for i in range(batch):
            e = pl.program_id(0) * batch + i
            for r in range(halves * pair):

                @pl.when(rank_ref[e] == r)
                def _(i=i, e=e, r=r):
                    lanes = slice((r % pair) * size, (r % pair + 1) * size)
                    for ref, height, start in zip(refs, heights, starts):
                        first = start + (r // pair) * height
                        out_ref[target_ref[e], first : first + height, lanes] = ref[i, :height]

    shape = (devices, total, pair * size)
    return call(
        body,
        "pack_blocks",
        (steps,),
        [pl.BlockSpec((batch, 16, size), lambda i, *_, g=g: (i, g, 0)) for g in groups],
        pl.BlockSpec(shape, lambda i, *_: (0, 0, 0)),
        jax.ShapeDtypeStruct(shape, BF),
        prefetch=2,
    )(target, rank, *([store] * len(groups)))


def spread_out(incoming, source, rank, mask, molecules, aux, capacity, groups):
    size = BO * BO
    pair = 2 if capacity > 1 else 1
    halves = (capacity + pair - 1) // pair
    heights = piece_rows(groups, aux)
    starts, _ = piece_starts(groups, aux, halves)
    rows = 16 * len(groups)

    def body(source_ref, rank_ref, mask_ref, in_ref, out_ref, first_ref, last_ref):
        a = pl.program_id(0)
        for g, (height, start) in enumerate(zip(heights, starts)):
            blocks = []
            for s in range(NN):
                e = a * NN + s
                block = in_ref[source_ref[e], start : start + height, :]
                for h in range(1, halves):
                    other = in_ref[source_ref[e], start + h * height : start + (h + 1) * height, :]
                    block = jnp.where(rank_ref[e] // pair == h, other, block)
                own = block[:, :size]
                if pair == 2:
                    own = jnp.where(rank_ref[e] % pair == 1, block[:, size:], own)
                blocks.append(jnp.where(mask_ref[e] == 1, own, jnp.zeros_like(own)))
            gap = jnp.zeros((height, LANE - NN * BO), BF)
            if height < 16:
                out_ref[0, g * 16 : (g + 1) * 16] = jnp.zeros((16, BO * LANE), BF)
            for mu in range(BO):
                parts = [b[:, mu * BO : (mu + 1) * BO] for b in blocks] + [gap]
                out_ref[0, g * 16 : g * 16 + height, mu * LANE : (mu + 1) * LANE] = jnp.concatenate(
                    parts, axis=1
                )

        @pl.when(a < HALF)
        def _():
            first_ref[...] = out_ref[...]

        @pl.when(a >= molecules - HALF)
        def _():
            last_ref[...] = out_ref[...]

    shape = (1, rows, BO * LANE)
    return call(
        body,
        "spread_out",
        (molecules,),
        [pl.BlockSpec(incoming.shape, lambda a, *_: (0, 0, 0))],
        [
            pl.BlockSpec(shape, lambda a, *_: (a, 0, 0)),
            pl.BlockSpec(shape, lambda a, *_: (jnp.minimum(a, HALF - 1), 0, 0)),
            pl.BlockSpec(shape, lambda a, *_: (jnp.maximum(a - (molecules - HALF), 0), 0, 0)),
        ],
        [
            jax.ShapeDtypeStruct((molecules, *shape[1:]), BF),
            jax.ShapeDtypeStruct((HALF, *shape[1:]), BF),
            jax.ShapeDtypeStruct((HALF, *shape[1:]), BF),
        ],
        prefetch=3,
    )(source, rank, mask, incoming)


def fold_kernel(own, virtual, occupied, widen):
    molecules, rows = own.shape[:2]
    units = occupied.shape[0]

    def body(own_ref, virtual_ref, occ_ref, widen_ref, x_ref, window_ref):
        u = pl.program_id(0)
        a = jnp.where(u < molecules, u, u - molecules)

        def place(slots):
            for t in range(NTAU):
                for s in range(NN):
                    row = virtual_ref[t, a + s].astype(F32)
                    for k, w in enumerate(slots):
                        off = (s - w) * BO
                        if off >= 0:
                            parts = [jnp.zeros((BO, off), F32)] * (off > 0) + [
                                row[:, : NN * BO - off],
                                jnp.zeros((BO, LANE - NN * BO), F32),
                            ]
                        else:
                            parts = [row[:, -off:], jnp.zeros((BO, LANE - NN * BO - off), F32)]
                        lanes = slice((t * KEPT + k) * LANE, (t * KEPT + k + 1) * LANE)
                        window_ref[s * BO : (s + 1) * BO, lanes] = jnp.concatenate(parts, axis=1)

        @pl.when(u == 0)
        def _():
            window_ref[NN * BO :] = jnp.zeros((LANE - NN * BO, NTAU * KEPT * LANE), F32)

        @pl.when(u < molecules)
        def _():
            place((2, 3, 4))

        @pl.when(u >= molecules)
        def _():
            place((0, 1, 1))

        window = window_ref[...].astype(BF)
        krons = []
        shape = (KEPT * BO, 8, BO * 8)
        keep = lax.broadcasted_iota(jnp.int32, shape, 2) % 8 == lax.broadcasted_iota(jnp.int32, shape, 1)
        for t in range(NTAU):
            wide = jnp.dot(occ_ref[0, t], widen_ref[...], preferred_element_type=F32)
            wide = jnp.where(keep, jnp.broadcast_to(wide[:, None, :], shape), 0.0)
            krons.append(wide.reshape(KEPT * BO * 8, BO * 8).astype(BF))
        for g in range(rows // 16):
            own_rows = jnp.concatenate(
                [
                    own_ref[0, g * 16 : (g + 1) * 16, mu * LANE : (mu + 1) * LANE]
                    for mu in range(BO)
                ],
                axis=0,
            )
            spread = jnp.dot(own_rows, window, preferred_element_type=F32)
            for t in range(NTAU):
                first = t * rows + g * 16
                for w in range(KEPT):
                    lane = (t * KEPT + w) * LANE
                    part = spread[:, lane : lane + LANE].reshape(BO, 2, 8, LANE)
                    part = jnp.concatenate(
                        [part[:, 0].reshape(BO * 8, LANE), part[:, 1].reshape(BO * 8, LANE)],
                        axis=1,
                    ).astype(BF)
                    folded = jnp.dot(
                        krons[t][w * BO * 8 : (w + 1) * BO * 8], part, preferred_element_type=F32
                    ).reshape(BO, 8, 2 * LANE)
                    folded = jnp.concatenate(
                        [folded[:, :, :LANE], folded[:, :, LANE:]], axis=1
                    ).astype(BF)
                    for el in range(BO):
                        x_ref[0, w, first : first + 16, el * LANE : (el + 1) * LANE] = folded[el]

    whole = lambda x: pl.BlockSpec(x.shape, lambda u: (0,) * x.ndim)
    shape = (KEPT, NTAU * rows, BO * LANE)
    return call(
        body,
        "fold",
        (units,),
        [
            pl.BlockSpec((1, *own.shape[1:]), lambda u: (jnp.where(u < molecules, u, u - molecules), 0, 0)),
            whole(virtual),
            pl.BlockSpec((1, *occupied.shape[1:]), lambda u: (u, 0, 0, 0)),
            whole(widen),
        ],
        pl.BlockSpec((1, *shape), lambda u: (u, 0, 0, 0)),
        jax.ShapeDtypeStruct((units, *shape), BF),
        [pltpu.VMEM((LANE, NTAU * KEPT * LANE), F32)],
    )(own, virtual, occupied, widen)


def runs_of(groups):
    runs = []
    for at, g in enumerate(groups):
        if runs and runs[-1][1] + runs[-1][2] == g:
            runs[-1][2] += 1
        else:
            runs.append([at, g, 1])
    return runs


def chi_kernel(parts, folded, chunks, aux):
    molecules = parts[0][1].shape[0]
    total = molecules + 2 * HALF
    rows = sum(16 * len(groups) for groups in chunks)
    count = sum(len(p) for p in parts)
    moves = []
    for c, groups in enumerate(chunks):
        for which, (first, much) in enumerate(
            ((0, HALF), (HALF, molecules), (HALF + molecules, HALF))
        ):
            for at, g, length in runs_of(groups):
                moves.append((c * 3 + which, first, much, at * 16, g * 16, length * 16))
    plan = sorted((g, c, at) for c, groups in enumerate(chunks) for at, g in enumerate(groups))

    def body(*refs):
        ins, xs = refs[:count], refs[count : count + KEPT * len(chunks)]
        out_ref, blocks_ref, all_ref, sem = refs[count + KEPT * len(chunks) :]
        q = pl.program_id(0)

        def copies():
            for i, (which, first, much, at, to, length) in enumerate(moves):
                yield pltpu.make_async_copy(
                    ins[which].at[:, at : at + length],
                    blocks_ref.at[first : first + much, to : to + length],
                    sem.at[i],
                )

        @pl.when(q == 0)
        def _():
            for copy in copies():
                copy.start()
            for copy in copies():
                copy.wait()

        near = blocks_ref[q]
        chis = []
        for k in range(KEPT):
            results = [
                lax.dot_general(
                    xs[k * len(chunks) + c][0, 0], near, (((1,), (1,)), ((), ())),
                    preferred_element_type=F32,
                )
                for c in range(len(chunks))
            ]
            both = []
            for t in range(NTAU):
                pieces = []
                for _, c, at in plan:
                    first = t * 16 * len(chunks[c]) + at * 16
                    pieces.append(results[c][first : first + 16])
                both.append(jnp.concatenate(pieces, axis=0))
            chis.append(both)

        def put(back, w, values):
            ring_at = (q + 4 - back) % 4
            for t in range(NTAU):
                all_ref[ring_at, pl.ds((w * NTAU + t) * rows, rows), :rows] = values[t]

        flip = lambda both: [jnp.transpose(x) for x in both]

        @pl.when(q == 0)
        def _():
            put(-2, 0, chis[0])

        @pl.when(q == 1)
        def _():
            put(-1, 1, chis[1])
            put(-2, 0, chis[0])

        @pl.when(q >= 2)
        def _():
            put(0, 2, chis[0])

        @pl.when(q >= 3)
        def _():
            put(1, 3, chis[1])
            put(0, 1, flip(chis[1]))

        @pl.when(q >= 4)
        def _():
            put(2, 4, chis[2])
            put(0, 0, flip(chis[2]))
            mine = (q + 2) % 4
            flat = jnp.concatenate(
                [
                    all_ref[mine, pl.ds(p, NN * NTAU, stride=rows), :][:, :aux]
                    for p in range(aux)
                ],
                axis=1,
            )
            for w in range(NN):
                out_ref[0, w] = flat[w * NTAU : (w + 1) * NTAU]

    last = molecules - 1

    def unit(k):
        def index(q):
            at = jnp.clip(q - HALF - k, 0, last)
            if k == 0:
                at = jnp.where(q < HALF, molecules + q, at)
            if k == 1:
                at = jnp.where(q == 1, molecules, at)
            return at, k, 0, 0

        return index

    out = call(
        body,
        "chi",
        (total,),
        [pl.BlockSpec(memory_space=pl.ANY)] * count
        + [
            pl.BlockSpec((1, 1, *x.shape[2:]), unit(k)) for k in range(KEPT) for x in folded
        ],
        pl.BlockSpec((1, NN, NTAU, aux * aux), lambda q: (jnp.maximum(q - 2 * HALF, 0), 0, 0, 0)),
        jax.ShapeDtypeStruct((molecules, NN, NTAU, aux * aux), F32),
        [
            pltpu.VMEM((total, rows, BO * LANE), BF),
            pltpu.VMEM((4, NN * NTAU * rows, LANE), F32),
            pltpu.SemaphoreType.DMA((len(moves),)),
        ],
    )(*[x for p in parts for x in p], *(list(folded) * KEPT))
    return jnp.transpose(out, (2, 0, 1, 3))


def ring(low, high):
    count = lax.axis_size("row")
    up = [(i, (i + 1) % count) for i in range(count)]
    down = [(j, i) for i, j in up]
    return lax.ppermute(low, "row", up), lax.ppermute(high, "row", down)


def green_operands(green, below, above):
    mol_dev = green.shape[2]
    virtual = jnp.concatenate([below, green[1], above], axis=1)
    virtual = virtual.reshape(NTAU, mol_dev + 2 * HALF, NN, BO, BO)
    virtual = jnp.transpose(virtual, (0, 1, 3, 2, 4))
    virtual = virtual.reshape(NTAU, mol_dev + 2 * HALF, BO, NN * BO)
    occupied = green[0].reshape(NTAU, mol_dev, NN, BO, BO)
    first = occupied[:, :HALF]
    first = jnp.stack([first[:, :, 0], first[:, :, 1], first[:, :, 1]], axis=2)
    occupied = jnp.concatenate([occupied[:, :, HALF:], first], axis=1)
    occupied = jnp.transpose(occupied, (1, 0, 2, 4, 3))
    return virtual, occupied.reshape(mol_dev + HALF, NTAU, KEPT * BO, BO)


def shards(b3_store, block_shift, green, block_mask):
    devices = lax.axis_size("row")
    myself = lax.axis_index("row")
    mol_dev, _, aux, size = b3_store.shape
    count = mol_dev * NN
    capacity = (count + devices - 1) // devices
    pair = 2 if capacity > 1 else 1
    halves = (capacity + pair - 1) // pair
    shifts = block_shift.reshape(count)
    position = jnp.arange(count, dtype=jnp.int32)
    same = (shifts[:, None] == shifts[None, :]) & (position[None, :] < position[:, None])
    rank = jnp.sum(same.astype(jnp.int32), axis=1)
    target = (myself - shifts) % devices
    anchor = (myself + shifts) % devices
    store = b3_store.reshape(count, aux, size)
    mask = block_mask.reshape(count)
    chunks = chunk_groups(aux)
    widen = jnp.asarray(np.repeat(np.eye(BO, dtype=np.float32), 8, axis=1), BF)

    outgoing = [pack_blocks(store, target, rank, devices, capacity, groups) for groups in chunks]
    held = green[1]
    below, above = ring(held[:, mol_dev - HALF :], held[:, :HALF])
    outgoing[0], below, above = lax.optimization_barrier((outgoing[0], below, above))
    virtual, occupied = green_operands(green, below, above)
    incoming = []
    for c in range(len(chunks)):
        incoming.append(lax.all_to_all(outgoing[c], "row", split_axis=0, concat_axis=0, tiled=True))
        if c == 0:
            incoming[0], virtual, occupied = lax.optimization_barrier((incoming[0], virtual, occupied))
        if c + 1 < len(chunks):
            incoming[c], outgoing[c + 1] = lax.optimization_barrier((incoming[c], outgoing[c + 1]))
    parts, folded = [], []
    for c, groups in enumerate(chunks):
        if c:
            rank, folded[c - 1] = lax.optimization_barrier((rank, folded[c - 1]))
        own, first, last = spread_out(
            incoming[c], anchor, rank, mask, mol_dev, aux, capacity, groups
        )
        above_and_below = ring(last, first)
        parts.append((above_and_below[0], own, above_and_below[1]))
        folded.append(fold_kernel(own, virtual, occupied, widen))
    return chi_kernel(parts, folded, chunks, aux)


def solution(mesh):
    in_specs = (
        P(("groups", "row"), None, None, None),
        P("groups", None),
        P(None, None, ("groups", "row"), None, None),
        P(("groups", "row"), None),
    )
    out_specs = P(None, ("groups", "row"), None, None)
    return jax.shard_map(shards, mesh=mesh, in_specs=in_specs, out_specs=out_specs, check_vma=False)
```

time: 933 us -> 226 us (0.24); the launches traced: 917 us -> 224 us
  local copies, waits for them, and re-layouts: 554 us -> 9.82 us
  matrix products: 194 us -> 0 us
  Pallas kernels: 0 us -> 113 us
  waiting for transfers between devices: 94.2 us -> 60.3 us
  loops' own time: 21.3 us -> 0 us
  other arithmetic: 17.5 us -> 2.67 us
    convert_element_type x13 -> x0, local copies, waits for them, and re-layouts: 203 us -> none  [the longest x6 184 us: molecule_chi(): folded.astype(jnp.bfloat16).reshape(aux_count, reach_slots, BO, NW, BO)]
    dot_general x42 -> x0, matrix products: 194 us -> none  [the longest x30 98.7 us: molecule_chi(): jnp.einsum('pluj,uqlj->pq', window_part, near_blocks[offset], preferred_e...]
    gather x43 -> x0, local copies, waits for them, and re-layouts: 126 us -> none  [the longest x3 52.8 us: molecule_chi(): lax.dynamic_slice_in_dim(partners, local_index, reach_slots, 0)]
    pallas_call x0 -> x7, Pallas kernels: none -> 113 us  [the longest x2 42.5 us: fold_kernel(): call(body, 'fold', (units,), [pl.BlockSpec((1, *own.shape[1:]), lambda u:...]
    slice x14 -> x5, local copies, waits for them, and re-layouts: 95.9 us -> 1.35 us  [the longest x1 1.25 us: green_operands(): occupied = green[0].reshape(NTAU, mol_dev, NN, BO, BO)]
    reshape x41 -> x3, local copies, waits for them, and re-layouts: 49.1 us -> 2.13 us  [the longest x1 1.38 us: green_operands(): virtual = virtual.reshape(NTAU, mol_dev + 2 * HALF, BO, NN * BO)]
    all_to_all x1 -> x2, waiting for transfers between devices: 94.2 us -> 60.3 us  [shards(): lax.all_to_all(outgoing[c], 'row', split_axis=0, concat_axis=0, tiled=True)]
    scatter x2 -> x0, local copies, waits for them, and re-layouts: 27.1 us -> none  [shards(): outgoing.at[target, slot_rank]]
  transfers between devices with their start and end apart: 5 -> 8, of which waited for: 1 -> 1; matrix products, arithmetic and copies ran while one was open for 4% -> 4% of each run, Pallas kernels for 0% -> 36%
where the time goes in v1:
time: 226 us; the launch traced here: 224 us
  Pallas kernels  113 us (50%)
  waiting for transfers between devices  60.3 us (27%)
  starting transfers between devices  38.4 us (17%)
  local copies, waits for them, and re-layouts  9.82 us (4%)
  other arithmetic  2.67 us (1%)
    all_to_all x2, waiting for transfers between devices, shards(): lax.all_to_all(outgoing[c], 'row', split_axis=0, concat_axis=0, tiled=True)  60.3 us
    pallas_call x2, Pallas kernels, fold_kernel(): call(body, 'fold', (units,), [pl.BlockSpec((1, *own.shape[1:]), lambda u:...  42.5 us
    pallas_call x1, Pallas kernels, chi_kernel(): call(body, 'chi', (total,), [pl.BlockSpec(memory_space=pl.ANY)] * count +...  31.7 us
    pallas_call x2, Pallas kernels, spread_out(): call(body, 'spread_out', (molecules,), [pl.BlockSpec(incoming.shape, lamb...  24.5 us
    all_to_all x2, starting transfers between devices, shards(): lax.all_to_all(outgoing[c], 'row', split_axis=0, concat_axis=0, tiled=True)  24.1 us
    ppermute x6, starting transfers between devices, ring(): return (lax.ppermute(low, 'row', up), lax.ppermute(high, 'row', down))  14.4 us
    pallas_call x2, Pallas kernels, pack_blocks(): call(body, 'pack_blocks', (steps,), [pl.BlockSpec((batch, 16, size), lamb...  14.2 us
  transfers between devices with their start and end apart: 8, of which 1 were waited for; matrix products, arithmetic and copies ran while one was open for 4% of the time, Pallas kernels for 36%

profile of v1, /device:TPU:0, one launch (start us, length us, event | category | flops | bytes accessed | tf_op | source)
XLA Modules:
  0.0 224.2 jit_solution(10755171767412854432)
XLA Ops:
  0.0 1.3 fusion.3
  1.3 5.5 %collective-permute-start.1 = (bf16[2,2,5,576]{3,0,2,1:T(2,128)(2,1)S(1)}, bf16[2,2,5,576]{3,0,2,1:T(2,128)(2,1)S(1)}, u32[]{:S(2)}, u32[]{:S(2)}) collective-permute-start(bf16[2,2,5,576]{3,0,2,1:T(2,128)(2,1)S(1)} %get-tuple-element.40), channel_id=1, source_target_pairs={{1,0},{2,1},{3,2},{4,3},{5,4},{6,5},{7,6},{8,7},{9,8},{10,9},{11,1... | collective-permute-start | bytes 69128 | tf_op jit(solution)/shard_map/ppermute | solution.py:378
  6.8 0.8 copy.22
  8.2 0.7 convert_reduce_fusion.rank_ref
  8.9 8.5 %pack_blocks.2 = bf16[16,104,1152]{2,1,0:T(8,128)(2,1)} custom-call(s32[60]{0:T(128)} %get-tuple-element.42.target_ref, s32[60]{0:T(128)} %convert_reduce_fusion.rank_ref, bf16[60,68,576]{2,1,0:T(8,128)(2,1)} %bitcast.17, bf16[60,68,576]{2,1,0:T(8,128)(2,1)} %bitcast.18, bf16[60,68,576]{2,1,0:T(8,128)(2,1)} %bitcast.19, bf16[60,68,576]{2,1,0:T(8,128)(2,1)} %bitcast.20), custom_call_target="tpu_custom_call" | custom-call | tf_op jit(solution)/shard_map/pack_blocks/pallas_call | solution.py:80
  17.5 5.9 %all-to-all-start = ((bf16[16,104,1152]{2,1,0:T(8,128)(2,1)}), bf16[16,104,1152]{2,1,0:T(8,128)(2,1)}, u32[]{:S(2)}, u32[]{:S(2)}) async-start(bf16[16,104,1152]{2,1,0:T(8,128)(2,1)} %pack_blocks.2), calls=%async_computation | async-start | bytes 7667712 | tf_op jit(solution)/shard_map/all_to_all | solution.py:421
  23.4 0.7 reshape_squeeze.3
  24.2 5.6 %pack_blocks.3 = bf16[16,32,1152]{2,1,0:T(8,128)(2,1)} custom-call(s32[60]{0:T(128)} %get-tuple-element.42.target_ref, s32[60]{0:T(128)} %convert_reduce_fusion.rank_ref, bf16[60,68,576]{2,1,0:T(8,128)(2,1)} %bitcast.21), custom_call_target="tpu_custom_call" | custom-call | tf_op jit(solution)/shard_map/pack_blocks/pallas_call | solution.py:80
  30.2 0.7 concatenate.14
  31.3 0.9 maximum_maximum_fusion
  33.1 1.4 reshape.25.virtual_ref
  34.5 60.3 %all-to-all-done.in_ref = bf16[16,104,1152]{2,1,0:T(8,128)(2,1)} async-done(((bf16[16,104,1152]{2,1,0:T(8,128)(2,1)}), bf16[16,104,1152]{2,1,0:T(8,128)(2,1)}, u32[]{:S(2)}, u32[]{:S(2)}) %all-to-all-start) | async-done | bytes 3833888 | tf_op jit(solution)/shard_map/all_to_all | solution.py:421
  94.8 18.2 %all-to-all-start.1 = ((bf16[16,32,1152]{2,1,0:T(8,128)(2,1)}), bf16[16,32,1152]{2,1,0:T(8,128)(2,1)S(1)}, u32[]{:S(2)}, u32[]{:S(2)}) async-start(bf16[16,32,1152]{2,1,0:T(8,128)(2,1)} %pack_blocks.3), calls=%async_computation.1 | async-start | bytes 2359296 | tf_op jit(solution)/shard_map/all_to_all | solution.py:421
  113.1 0.7 reshape.23.mask_ref
  113.7 16.3 %spread_out.2 = (bf16[12,64,3072]{2,1,0:T(8,128)(2,1)}, bf16[2,64,3072]{2,1,0:T(8,128)(2,1)}, bf16[2,64,3072]{2,1,0:T(8,128)(2,1)}) custom-call(s32[60]{0:T(128)} %get-tuple-element.43.source_ref, s32[60]{0:T(128)} %convert_reduce_fusion.rank_ref, s32[60]{0:T(128)} %reshape.23.mask_ref, bf16[16,104,1152]{2,1,0:T(8,128)(2,1)} %all-to-all-done.in_ref), custom_call_target="tpu_custom_call" | custom-call | tf_op jit(solution)/shard_map/spread_out/pallas_call | solution.py:131
  130.5 4.0 %collective-permute-start.3 = (bf16[2,64,3072]{2,1,0:T(8,128)(2,1)}, bf16[2,64,3072]{2,1,0:T(8,128)(2,1)S(1)}, u32[]{:S(2)}, u32[]{:S(2)}) collective-permute-start(bf16[2,64,3072]{2,1,0:T(8,128)(2,1)} %get-tuple-element.28), channel_id=1, source_target_pairs={{1,0},{2,1},{3,2},{4,3},{5,4},{6,5},{7,6},{8,7},{9,8},{10,9},{11,1... | collective-permute-start | bytes 2359304 | tf_op jit(solution)/shard_map/ppermute | solution.py:378
  134.5 28.7 %fold.2.refs_6_.refs_8_.refs_10_ = bf16[14,3,128,3072]{3,2,1,0:T(8,128)(2,1)} custom-call(bf16[12,64,3072]{2,1,0:T(8,128)(2,1)} %get-tuple-element.27.own_ref.refs_1_, bf16[2,16,24,120]{3,2,1,0:T(8,128)(2,1)} %reshape.25.virtual_ref, bf16[14,2,72,24]{3,2,1,0:T(8,128)(2,1)} %bitcast.22, bf16[24,192]{1,0:T(8,128)(2,1)} %constant.27.clone.widen_ref), custom_call_target="tpu_custom_call" | custom-call | tf_op jit(solution)/shard_map/fold/pallas_call | solution.py:223
  163.2 1.0 copy-done
  164.2 8.1 %spread_out.3 = (bf16[12,16,3072]{2,1,0:T(8,128)(2,1)}, bf16[2,16,3072]{2,1,0:T(8,128)(2,1)}, bf16[2,16,3072]{2,1,0:T(8,128)(2,1)}) custom-call(s32[60]{0:T(128)} %get-tuple-element.43.source_ref, s32[60]{0:T(128)} %convert_reduce_fusion.rank_ref, s32[60]{0:T(128)} %reshape.23.mask_ref, bf16[16,32,1152]{2,1,0:T(8,128)(2,1)} %copy-done), custom_call_target="tpu_custom_call" | custom-call | tf_op jit(solution)/shard_map/spread_out/pallas_call | solution.py:131
  172.3 4.4 %collective-permute-start.5 = (bf16[2,16,3072]{2,1,0:T(8,128)(2,1)}, bf16[2,16,3072]{2,1,0:T(8,128)(2,1)S(1)}, u32[]{:S(2)}, u32[]{:S(2)}) collective-permute-start(bf16[2,16,3072]{2,1,0:T(8,128)(2,1)} %get-tuple-element.35), channel_id=1, source_target_pairs={{1,0},{2,1},{3,2},{4,3},{5,4},{6,5},{7,6},{8,7},{9,8},{10,9},{11,1... | collective-permute-start | bytes 589832 | tf_op jit(solution)/shard_map/ppermute | solution.py:378
  176.8 13.9 %fold.3.refs_7_.refs_9_.refs_11_ = bf16[14,3,32,3072]{3,2,1,0:T(8,128)(2,1)} custom-call(bf16[12,16,3072]{2,1,0:T(8,128)(2,1)} %get-tuple-element.34.own_ref.refs_4_, bf16[2,16,24,120]{3,2,1,0:T(8,128)(2,1)} %reshape.25.virtual_ref, bf16[14,2,72,24]{3,2,1,0:T(8,128)(2,1)} %bitcast.23, bf16[24,192]{1,0:T(8,128)(2,1)} %constant.27.clone.widen_ref), custom_call_target="tpu_custom_call" | custom-call | tf_op jit(solution)/shard_map/fold/pallas_call | solution.py:223
  190.7 0.8 copy-done.1
  191.9 0.7 copy-done.4
  192.5 31.7 %chi.1 = f32[12,5,2,4624]{3,2,1,0:T(2,128)} custom-call(bf16[2,64,3072]{2,1,0:T(8,128)(2,1)} %copy-done.1, bf16[12,64,3072]{2,1,0:T(8,128)(2,1)} %get-tuple-element.27.own_ref.refs_1_, bf16[2,64,3072]{2,1,0:T(8,128)(2,1)} %copy-done.2, bf16[2,16,3072]{2,1,0:T(8,128)(2,1)} %copy-done.3, bf16[12,16,3072]{2,1,0:T(8,128)(2,1)} %get-tuple-element.34.own_ref.refs_4_, ...), custom_call_target="tpu_custom_call" | custom-call | tf_op jit(solution)/shard_map/chi/pallas_call | solution.py:355
  (35 shorter events, 3.3 us)
Async XLA Ops:
  1.3 16.2 %collective-permute-start.1 = (bf16[2,2,5,576]{3,0,2,1:T(2,128)(2,1)S(1)}, bf16[2,2,5,576]{3,0,2,1:T(2,128)(2,1)S(1)}, u32[]{:S(2)}, u32[]{:S(2)}) collective-permute-start(bf16[2,2,5,576]{3,0,2,1:T(2,128)(2,1)S(1)} %get-tuple-element.40), channel_id=1, source_target_pairs={{1,0},{2,1},{3,2},{4,3},{5,4},{6,5},{7,6},{8,7},{9,8},{10,9},{11,1... | collective-permute-start | bytes 69128 | tf_op jit(solution)/shard_map/ppermute | solution.py:378
  6.8 10.7 %collective-permute-start = (bf16[2,2,5,576]{3,0,2,1:T(2,128)(2,1)S(1)}, bf16[2,2,5,576]{3,0,2,1:T(2,128)(2,1)S(1)}, u32[]{:S(2)}, u32[]{:S(2)}) collective-permute-start(bf16[2,2,5,576]{3,0,2,1:T(2,128)(2,1)S(1)} %get-tuple-element.41), channel_id=1, source_target_pairs={{0,1},{1,2},{2,3},{3,4},{4,5},{5,6},{6,7},{7,8},{8,9},{9,10},{10,1... | collective-permute-start | bytes 69128 | tf_op jit(solution)/shard_map/ppermute | solution.py:378
  17.5 77.3 %all-to-all-start = ((bf16[16,104,1152]{2,1,0:T(8,128)(2,1)}), bf16[16,104,1152]{2,1,0:T(8,128)(2,1)}, u32[]{:S(2)}, u32[]{:S(2)}) async-start(bf16[16,104,1152]{2,1,0:T(8,128)(2,1)} %pack_blocks.2), calls=%async_computation | async-start | bytes 7667712 | tf_op jit(solution)/shard_map/all_to_all | solution.py:421
  34.5 78.5 %copy-start.5 = (s32[12,5]{0,1:T(8,128)S(1)}, s32[12,5]{0,1:T(8,128)}, u32[]{:S(2)}) copy-start(s32[12,5]{0,1:T(8,128)} %param.8) | copy-start | bytes 724
  94.8 68.4 %all-to-all-start.1 = ((bf16[16,32,1152]{2,1,0:T(8,128)(2,1)}), bf16[16,32,1152]{2,1,0:T(8,128)(2,1)S(1)}, u32[]{:S(2)}, u32[]{:S(2)}) async-start(bf16[16,32,1152]{2,1,0:T(8,128)(2,1)} %pack_blocks.3), calls=%async_computation.1 | async-start | bytes 2359296 | tf_op jit(solution)/shard_map/all_to_all | solution.py:421
  130.1 60.6 %collective-permute-start.2 = (bf16[2,64,3072]{2,1,0:T(8,128)(2,1)}, bf16[2,64,3072]{2,1,0:T(8,128)(2,1)S(1)}, u32[]{:S(2)}, u32[]{:S(2)}) collective-permute-start(bf16[2,64,3072]{2,1,0:T(8,128)(2,1)} %get-tuple-element.26), channel_id=1, source_target_pairs={{0,1},{1,2},{2,3},{3,4},{4,5},{5,6},{6,7},{7,8},{8,9},{9,10},{10,1... | collective-permute-start | bytes 2359304 | tf_op jit(solution)/shard_map/ppermute | solution.py:378
  130.5 60.2 %collective-permute-start.3 = (bf16[2,64,3072]{2,1,0:T(8,128)(2,1)}, bf16[2,64,3072]{2,1,0:T(8,128)(2,1)S(1)}, u32[]{:S(2)}, u32[]{:S(2)}) collective-permute-start(bf16[2,64,3072]{2,1,0:T(8,128)(2,1)} %get-tuple-element.28), channel_id=1, source_target_pairs={{1,0},{2,1},{3,2},{4,3},{5,4},{6,5},{7,6},{8,7},{9,8},{10,9},{11,1... | collective-permute-start | bytes 2359304 | tf_op jit(solution)/shard_map/ppermute | solution.py:378
  163.2 1.0 copy-start
  172.3 18.3 %collective-permute-start.4 = (bf16[2,16,3072]{2,1,0:T(8,128)(2,1)}, bf16[2,16,3072]{2,1,0:T(8,128)(2,1)S(1)}, u32[]{:S(2)}, u32[]{:S(2)}) collective-permute-start(bf16[2,16,3072]{2,1,0:T(8,128)(2,1)} %get-tuple-element.33), channel_id=1, source_target_pairs={{0,1},{1,2},{2,3},{3,4},{4,5},{5,6},{6,7},{7,8},{8,9},{9,10},{10,1... | collective-permute-start | bytes 589832 | tf_op jit(solution)/shard_map/ppermute | solution.py:378
  172.3 18.4 %collective-permute-start.5 = (bf16[2,16,3072]{2,1,0:T(8,128)(2,1)}, bf16[2,16,3072]{2,1,0:T(8,128)(2,1)S(1)}, u32[]{:S(2)}, u32[]{:S(2)}) collective-permute-start(bf16[2,16,3072]{2,1,0:T(8,128)(2,1)} %get-tuple-element.35), channel_id=1, source_target_pairs={{1,0},{2,1},{3,2},{4,3},{5,4},{6,5},{7,6},{8,7},{9,8},{10,9},{11,1... | collective-permute-start | bytes 589832 | tf_op jit(solution)/shard_map/ppermute | solution.py:378
  190.6 0.9 copy-start.1
  190.6 1.2 copy-start.2
  190.7 1.2 copy-start.3
  191.9 0.7 copy-start.4

commit v2 on v1

v2 whole, which is shorter than its diff:
```python
import functools

import jax
import jax.numpy as jnp
import numpy as np
from jax import lax
from jax.experimental import pallas as pl
from jax.experimental.pallas import tpu as pltpu
from jax.sharding import PartitionSpec as P

BO = 24
HALF = 2
NTAU = 2
NN = 5
NW = 9
LANE = 128
KEPT = 3
BF = jnp.bfloat16
F32 = jnp.float32
VMEM_LIMIT = 56 * 1024 * 1024


def call(body, name, grid, in_specs, out_specs, out_shape, scratch=(), prefetch=0):
    return pl.pallas_call(
        body,
        grid_spec=pltpu.PrefetchScalarGridSpec(
            num_scalar_prefetch=prefetch,
            grid=grid,
            in_specs=in_specs,
            out_specs=out_specs,
            scratch_shapes=list(scratch),
        ),
        out_shape=out_shape,
        name=name,
        compiler_params=pltpu.CompilerParams(vmem_limit_bytes=VMEM_LIMIT),
    )


def chunk_groups(aux):
    full = aux // 16
    last = [full] if aux % 16 else []
    return [list(range(full - 1)), [full - 1] + last]


def piece_rows(groups, aux):
    return [min(16, aux - 16 * g) for g in groups]


def piece_starts(groups, aux, halves):
    starts, row = [], 0
    for height in piece_rows(groups, aux):
        starts.append(row)
        row += height * halves
    return starts, row


def pack_blocks(store, target, rank, devices, capacity, groups):
    count, aux, size = store.shape
    pair = 2 if capacity > 1 else 1
    halves = (capacity + pair - 1) // pair
    heights = piece_rows(groups, aux)
    starts, total = piece_starts(groups, aux, halves)
    steps = 4
    batch = count // steps
    bulk = size // LANE * LANE
    rest = size - bulk

    def body(target_ref, rank_ref, *refs):
        out_ref = refs[-1]
        for i in range(batch):
            e = pl.program_id(0) * batch + i
            for r in range(halves * pair):

                @pl.when(rank_ref[e] == r)
                def _(i=i, e=e, r=r):
                    for ref, height, start in zip(refs, heights, starts):
                        first = start + (r // pair) * height
                        at = (target_ref[e], slice(first, first + height))
                        if r % pair:
                            out_ref[(*at, slice(size, size + rest))] = ref[i, :height, bulk:]
                            out_ref[(*at, slice(size + rest, None))] = ref[i, :height, :bulk]
                        else:
                            out_ref[(*at, slice(0, size))] = ref[i, :height]

    shape = (devices, total, pair * size)
    return call(
        body,
        "pack_blocks",
        (steps,),
        [pl.BlockSpec((batch, 16, size), lambda i, *_, g=g: (i, g, 0)) for g in groups],
        pl.BlockSpec(shape, lambda i, *_: (0, 0, 0)),
        jax.ShapeDtypeStruct(shape, BF),
        prefetch=2,
    )(target, rank, *([store] * len(groups)))


def regroup_tables(pair):
    size = BO * BO
    tables = []
    for at in range(0, size, LANE):
        width = min(LANE, size - at)
        first, last = at // BO, (at + width - 1) // BO
        table = np.zeros((NN, LANE, last - first + 1, LANE), np.float32)
        for lane in range(width):
            mu, i = divmod(at + lane, BO)
            for s in range(NN):
                table[s, lane, mu - first, s * BO + i] = 1
                if width < LANE and pair == 2:
                    table[s, lane + width, mu - first, s * BO + i] = 1
        tables.append((first, last, table.reshape(NN * LANE, -1)))
    return tables


def spread_out(incoming, source, rank, mask, aux, capacity, groups):
    size = BO * BO
    pair = 2 if capacity > 1 else 1
    halves = (capacity + pair - 1) // pair
    heights = piece_rows(groups, aux)
    starts, _ = piece_starts(groups, aux, halves)
    rows = 16 * len(groups)
    bulk = size // LANE * LANE
    rest = size - bulk
    tables = regroup_tables(pair)
    molecules = source.shape[0] // NN
    per_step = next(n for n in (6, 4, HALF) if molecules % n == 0)
    steps = molecules // per_step

    def body(source_ref, rank_ref, mask_ref, in_ref, *refs):
        table_refs = refs[: len(tables)]
        out_ref, first_ref, last_ref = refs[len(tables) :]
        step = pl.program_id(0)
        lane = lax.broadcasted_iota(jnp.int32, (16, LANE), 1)
        stretches = [[] for _ in tables]
        for i in range(per_step):
            a = step * per_step + i
            for height, start in zip(heights, starts):
                tiles = [[] for _ in tables]
                for s in range(NN):
                    e = a * NN + s
                    half, odd = rank_ref[e] // pair, rank_ref[e] % pair
                    if height == 16:
                        rows_at = pl.ds(pl.multiple_of(start + half * 16, 16), 16)
                        lanes_at = pl.ds(pl.multiple_of(odd * (size + rest), LANE), bulk)
                        main = in_ref[source_ref[e], rows_at, lanes_at]
                        tail = in_ref[source_ref[e], rows_at, bulk : bulk + pair * rest]
                    else:
                        both = in_ref[source_ref[e], start : start + halves * height, :].astype(F32)
                        picked = both[:height]
                        for h in range(1, halves):
                            picked = jnp.where(half == h, both[h * height : (h + 1) * height], picked)
                        gap = jnp.zeros((16 - height, picked.shape[1]), F32)
                        picked = jnp.concatenate([picked, gap], axis=0).astype(BF)
                        main, tail = picked[:, :bulk], picked[:, bulk : bulk + pair * rest]
                        if pair == 2:
                            main = jnp.where(odd == 1, picked[:, size + rest :], main)
                    kept = jnp.full((16, LANE), mask_ref[e], jnp.int32)
                    if pair == 2:
                        here = jnp.where((lane >= rest) == (odd == 1), kept, 0)
                    else:
                        here = kept
                        tail = jnp.concatenate([tail, jnp.zeros((16, LANE - rest), BF)], axis=1)
                    kept, here = kept.astype(F32).astype(BF), here.astype(F32).astype(BF)
                    for n in range(len(tables) - 1):
                        tiles[n].append(main[:, n * LANE : (n + 1) * LANE] * kept)
                    tiles[-1].append(tail * here)
                for n in range(len(tables)):
                    stretches[n].append(jnp.concatenate(tiles[n], axis=1))
        carried = None
        for n, (first, last, _) in enumerate(tables):
            moved = jnp.dot(
                jnp.concatenate(stretches[n], axis=0), table_refs[n][...], preferred_element_type=F32
            )
            shared = n + 1 < len(tables) and tables[n + 1][0] == last
            for mu in range(first, last + 1):
                tile = moved[:, (mu - first) * LANE : (mu - first + 1) * LANE]
                if mu == first and carried is not None:
                    tile = tile + carried
                if mu == last and shared:
                    carried = tile
                else:
                    out_ref[:, :, mu * LANE : (mu + 1) * LANE] = tile.astype(BF).reshape(
                        per_step, rows, LANE
                    )
            if not shared:
                carried = None

        @pl.when(step == 0)
        def _():
            first_ref[...] = out_ref[:HALF]

        @pl.when(step == steps - 1)
        def _():
            last_ref[...] = out_ref[per_step - HALF :]

    shape = (rows, BO * LANE)
    return call(
        body,
        "spread_out",
        (steps,),
        [pl.BlockSpec(incoming.shape, lambda a, *_: (0, 0, 0))]
        + [pl.BlockSpec(t.shape, lambda a, *_: (0, 0)) for _, _, t in tables],
        [
            pl.BlockSpec((per_step, *shape), lambda a, *_: (a, 0, 0)),
            pl.BlockSpec((HALF, *shape), lambda a, *_: (0, 0, 0)),
            pl.BlockSpec((HALF, *shape), lambda a, *_: (0, 0, 0)),
        ],
        [
            jax.ShapeDtypeStruct((molecules, *shape), BF),
            jax.ShapeDtypeStruct((HALF, *shape), BF),
            jax.ShapeDtypeStruct((HALF, *shape), BF),
        ],
        prefetch=3,
    )(source, rank, mask, incoming, *[jnp.asarray(t, BF) for _, _, t in tables])


def place_windows(virtual_ref, a, slots, window_ref):
    for t in range(NTAU):
        for s in range(NN):
            row = virtual_ref[a + s, t].astype(F32)
            for k, w in enumerate(slots):
                off = (s - w) * BO
                if off >= 0:
                    parts = [jnp.zeros((BO, off), F32)] * (off > 0) + [
                        row[:, : NN * BO - off],
                        jnp.zeros((BO, LANE - NN * BO), F32),
                    ]
                else:
                    parts = [row[:, -off:], jnp.zeros((BO, LANE - NN * BO - off), F32)]
                lanes = slice((t * KEPT + k) * LANE, (t * KEPT + k + 1) * LANE)
                window_ref[s * BO : (s + 1) * BO, lanes] = jnp.concatenate(parts, axis=1)


def join(refs, to_ref):
    at = 0
    for ref in refs:
        to_ref[at : at + ref.shape[0]] = ref[...]
        at += ref.shape[0]


def set_windows(u, a, virtual_ref, window_ref):
    @pl.when(u == 0)
    def _():
        window_ref[NN * BO :] = jnp.zeros((LANE - NN * BO, NTAU * KEPT * LANE), F32)

    @pl.when(u < HALF)
    def _():
        place_windows(virtual_ref, a, (0, 1, 1), window_ref)

    @pl.when(u >= HALF)
    def _():
        place_windows(virtual_ref, a, (2, 3, 4), window_ref)


def fold_unit(own, groups, window, occ_ref, widen, put):
    krons = []
    shape = (KEPT * BO, 8, BO * 8)
    keep = lax.broadcasted_iota(jnp.int32, shape[1:], 1) % 8 == lax.broadcasted_iota(jnp.int32, shape[1:], 0)
    keep = keep.astype(F32)[None]
    for t in range(NTAU):
        wide = jnp.dot(occ_ref[0, t], widen, preferred_element_type=F32)
        krons.append((wide[:, None, :] * keep).reshape(KEPT * BO * 8, BO * 8).astype(BF))
    part_rows = BO * 16 // 4
    for g in range(groups):
        rows = own(g)
        pieces = [[] for _ in range(NTAU * KEPT)]
        for p in range(0, NTAU * KEPT, 2):
            for first in range(0, BO * 16, part_rows):
                spread = jnp.dot(
                    rows[first : first + part_rows],
                    window[:, p * LANE : (p + 2) * LANE],
                    preferred_element_type=F32,
                )
                for z in range(2):
                    part = spread[:, z * LANE : (z + 1) * LANE].reshape(part_rows // 16, 2, 8, LANE)
                    part = [part[:, h].reshape(part_rows // 2, LANE) for h in range(2)]
                    pieces[p + z].append(jnp.concatenate(part, axis=1).astype(BF))
        for t in range(NTAU):
            for w in range(KEPT):
                part = jnp.concatenate(pieces[t * KEPT + w], axis=0)
                folded = jnp.dot(
                    krons[t][w * BO * 8 : (w + 1) * BO * 8], part, preferred_element_type=F32
                ).reshape(BO, 8, 2 * LANE)
                folded = jnp.concatenate([folded[:, :, :LANE], folded[:, :, LANE:]], axis=1).astype(BF)
                for el in range(BO):
                    put(w, t, g, el, folded[el])


def fold_kernel(own, virtual, occupied, widen):
    molecules, rows = own.shape[:2]
    units = occupied.shape[0]

    def body(own_ref, low_ref, mid_ref, high_ref, occ_ref, widen_ref, x_ref, window_ref, virtual_ref):
        u = pl.program_id(0)

        @pl.when(u == 0)
        def _():
            join((low_ref, mid_ref, high_ref), virtual_ref)

        set_windows(u, jnp.where(u < HALF, u, u - HALF), virtual_ref, window_ref)

        def rows_of(g):
            return jnp.concatenate(
                [
                    own_ref[0, g * 16 : (g + 1) * 16, mu * LANE : (mu + 1) * LANE]
                    for mu in range(BO)
                ],
                axis=0,
            )

        def put(w, t, g, el, tile):
            first = t * rows + g * 16
            x_ref[0, w, first : first + 16, el * LANE : (el + 1) * LANE] = tile

        fold_unit(rows_of, rows // 16, window_ref[...].astype(BF), occ_ref, widen_ref[...], put)

    whole = lambda x: pl.BlockSpec(x.shape, lambda u: (0,) * x.ndim)
    shape = (KEPT, NTAU * rows, BO * LANE)
    return call(
        body,
        "fold",
        (units,),
        [
            pl.BlockSpec((1, *own.shape[1:]), lambda u: (jnp.where(u < HALF, u, u - HALF), 0, 0)),
            *[whole(v) for v in virtual],
            pl.BlockSpec((1, *occupied.shape[1:]), lambda u: (u, 0, 0, 0)),
            whole(widen),
        ],
        pl.BlockSpec((1, *shape), lambda u: (u, 0, 0, 0)),
        jax.ShapeDtypeStruct((units, *shape), BF),
        [
            pltpu.VMEM((LANE, NTAU * KEPT * LANE), F32),
            pltpu.VMEM((units + HALF, NTAU, BO, NN * BO), BF),
        ],
    )(own, *virtual, occupied, widen)


def runs_of(groups):
    runs = []
    for at, g in enumerate(groups):
        if runs and runs[-1][1] + runs[-1][2] == g:
            runs[-1][2] += 1
        else:
            runs.append([at, g, 1])
    return runs


def row_plan(chunks):
    heights = [16 * len(groups) for groups in chunks]
    below = [NTAU * sum(heights[:c]) for c in range(len(chunks))]
    spots = sorted((g, c, at) for c, groups in enumerate(chunks) for at, g in enumerate(groups))
    plan = [[below[c] + t * heights[c] + at * 16 for _, c, at in spots] for t in range(NTAU)]
    return heights, below, plan


def in_order(result, plan):
    return [jnp.concatenate([result[at : at + 16] for at in spots], axis=0) for spots in plan]


def flatten(all_ref, at, count, rows, aux):
    return jnp.concatenate(
        [all_ref[at, pl.ds(p, count, stride=rows), :][:, :aux] for p in range(aux)], axis=1
    )


def chi_kernel(parts, folded, virtual, occupied, widen, chunks, aux):
    molecules = parts[0].shape[0]
    heights, below, plan = row_plan(chunks)
    rows = sum(heights)
    units = molecules + HALF
    head = 2
    ready = len(folded)
    moves = [
        (c, first, much, at * 16, g * 16, length * 16)
        for first, much in ((0, head), (head, molecules - head))
        for c, groups in enumerate(chunks)
        for at, g, length in runs_of(groups)
    ]

    def body(*refs):
        ins, xs = refs[: len(parts)], refs[len(parts) : len(parts) + ready]
        virtual_refs = refs[len(parts) + ready :][:3]
        occ_ref, widen_ref, out_ref, edge_ref = refs[len(parts) + ready + 3 :][:4]
        (blocks_ref, all_ref, x_ref, window_ref, virtual_ref, sem, x_sem, edge_sem) = refs[
            len(parts) + ready + 7 :
        ]
        q = pl.program_id(0)

        def loads(which):
            for i, (c, first, much, at, to, length) in enumerate(moves):
                if (first > 0) == which:
                    yield pltpu.make_async_copy(
                        ins[c].at[first : first + much, at : at + length],
                        blocks_ref.at[first : first + much, to : to + length],
                        sem.at[i],
                    )

        def fetch(step, c):
            return pltpu.make_async_copy(
                xs[c].at[step],
                x_ref.at[step % 4, :, below[c] : below[c] + NTAU * heights[c]],
                x_sem.at[c, step % 2],
            )

        def give(at, ring_at, k, i):
            return pltpu.make_async_copy(x_ref.at[ring_at, k], edge_ref.at[at], edge_sem.at[i])

        @pl.when(q == 0)
        def _():
            for copy in loads(False):
                copy.start()
            for c in range(ready):
                fetch(q, c).start()
            for copy in loads(True):
                copy.start()
            join(virtual_refs, virtual_ref)
            for copy in loads(False):
                copy.wait()

        @pl.when(q == HALF + head)
        def _():
            for copy in loads(True):
                copy.wait()

        @pl.when(q + 1 < units)
        def _():
            for c in range(ready):
                fetch(q + 1, c).start()

        @pl.when(q < units)
        def _():
            mine = jnp.where(q < HALF, q, q - HALF)
            set_windows(q, mine, virtual_ref, window_ref)
            last = chunks[-1]

            def rows_of(g):
                return jnp.concatenate(
                    [
                        blocks_ref[
                            mine, last[g] * 16 : (last[g] + 1) * 16, mu * LANE : (mu + 1) * LANE
                        ]
                        for mu in range(BO)
                    ],
                    axis=0,
                )

            def put(w, t, g, el, tile):
                first = below[-1] + t * heights[-1] + g * 16
                x_ref[q % 4, w, first : first + 16, el * LANE : (el + 1) * LANE] = tile

            fold_unit(rows_of, len(last), window_ref[...].astype(BF), occ_ref, widen_ref[...], put)
            for c in range(ready):
                fetch(q, c).wait()

        gifts = ((0, 0, 0), (0, 1, 1), (1, 2, 0), (units - 2, 3, 2), (units - 1, 4, 1), (units - 1, 5, 2))
        for i, (step, at, k) in enumerate(gifts):

            @pl.when(q == step)
            def _(i=i, step=step, at=at, k=k):
                give(at, step % 4, k, i).start()

        def chi(k):
            result = lax.dot_general(
                x_ref[(q + 4 - k) % 4, k], blocks_ref[q - HALF], (((1,), (1,)), ((), ())),
                preferred_element_type=F32,
            )
            return in_order(result, plan)

        def put_chi(back, w, values):
            ring_at = (q + 4 - back) % 4
            for t in range(NTAU):
                all_ref[ring_at, pl.ds((w * NTAU + t) * rows, rows), :rows] = values[t]

        def with_own():
            put_chi(0, 2, chi(0))

        def with_next():
            values = chi(1)
            put_chi(1, 3, values)
            put_chi(0, 1, [jnp.transpose(x) for x in values])

        def with_second():
            values = chi(2)
            put_chi(2, 4, values)
            put_chi(0, 0, [jnp.transpose(x) for x in values])

        def write():
            flat = flatten(all_ref, (q + 2) % 4, NN * NTAU, rows, aux)
            for w in range(NN):
                out_ref[0, w] = flat[w * NTAU : (w + 1) * NTAU]

        @pl.when(q == 2)
        def _():
            with_own()

        @pl.when(q == 3)
        def _():
            with_own()
            with_next()

        @pl.when((q >= 4) & (q < units))
        def _():
            with_own()
            with_next()
            with_second()
            write()

        @pl.when(q >= units)
        def _():
            write()

        for i, (step, at, k) in enumerate(gifts):

            @pl.when(q == step)
            def _(i=i, step=step, at=at, k=k):
                give(at, step % 4, k, i).wait()

    whole = lambda x: pl.BlockSpec(x.shape, lambda q: (0,) * x.ndim)
    x_shape = (NTAU * rows, BO * LANE)
    return call(
        body,
        "chi",
        (units + HALF,),
        [pl.BlockSpec(memory_space=pl.ANY)] * (len(parts) + ready)
        + [
            *[whole(v) for v in virtual],
            pl.BlockSpec((1, *occupied.shape[1:]), lambda q: (jnp.minimum(q, units - 1), 0, 0, 0)),
            whole(widen),
        ],
        [
            pl.BlockSpec((1, NN, NTAU, aux * aux), lambda q: (jnp.maximum(q - 2 * HALF, 0), 0, 0, 0)),
            pl.BlockSpec(memory_space=pl.ANY),
        ],
        [
            jax.ShapeDtypeStruct((molecules, NN, NTAU, aux * aux), F32),
            jax.ShapeDtypeStruct((6, *x_shape), BF),
        ],
        [
            pltpu.VMEM((molecules, rows, BO * LANE), BF),
            pltpu.VMEM((4, NN * NTAU * rows, LANE), F32),
            pltpu.VMEM((4, KEPT, *x_shape), BF),
            pltpu.VMEM((LANE, NTAU * KEPT * LANE), F32),
            pltpu.VMEM((units + HALF, NTAU, BO, NN * BO), BF),
            pltpu.SemaphoreType.DMA((len(moves),)),
            pltpu.SemaphoreType.DMA((max(ready, 1), 2)),
            pltpu.SemaphoreType.DMA((6,)),
        ],
    )(*parts, *folded, *virtual, occupied, widen)


def edge_kernel(chi, edge, halos, chunks, aux):
    molecules = chi.shape[0]
    heights, _, plan = row_plan(chunks)
    rows = sum(heights)
    place = np.array([[0, 0, 1, molecules - 2, molecules - 1, molecules - 1], [0, 1, 0, 4, 3, 4]], np.int32)
    spots = sorted((g, c, at) for c, groups in enumerate(chunks) for at, g in enumerate(groups))
    flat_halos = [h for side in halos for h in side]

    def body(edge_ref, *refs):
        below_refs, above_refs = refs[: len(chunks)], refs[len(chunks) : 2 * len(chunks)]
        out_ref, all_ref, flat_ref, sem = refs[2 * len(chunks) + 1 :]
        e = pl.program_id(0)

        def take(side, i):
            near = jnp.concatenate([side[c][i, at * 16 : (at + 1) * 16] for _, c, at in spots], axis=0)
            result = lax.dot_general(
                edge_ref[0], near, (((1,), (1,)), ((), ())), preferred_element_type=F32
            )
            for t, values in enumerate(in_order(result, plan)):
                all_ref[0, pl.ds((e * NTAU + t) * rows, rows), :rows] = values

        @pl.when(e < 3)
        def _():
            take(below_refs, jnp.minimum(e, 1))

        @pl.when(e >= 3)
        def _():
            take(above_refs, jnp.maximum(e - 4, 0))

        @pl.when(e == 5)
        def _():
            flat = flatten(all_ref, 0, 6 * NTAU, rows, aux)
            copies = []
            for i in range(6):
                flat_ref[i] = flat[i * NTAU : (i + 1) * NTAU]
                copies.append(
                    pltpu.make_async_copy(
                        flat_ref.at[i], out_ref.at[int(place[0, i]), int(place[1, i])], sem.at[i]
                    )
                )
                copies[-1].start()
            for copy in copies:
                copy.wait()

    return pl.pallas_call(
        body,
        grid=(6,),
        in_specs=[
            pl.BlockSpec((1, *edge.shape[1:]), lambda e: (e, 0, 0)),
            *[pl.BlockSpec(h.shape, lambda e: (0, 0, 0)) for h in flat_halos],
            pl.BlockSpec(memory_space=pl.ANY),
        ],
        out_specs=pl.BlockSpec(memory_space=pl.ANY),
        scratch_shapes=[
            pltpu.VMEM((1, 6 * NTAU * rows, LANE), F32),
            pltpu.VMEM((6, NTAU, aux * aux), F32),
            pltpu.SemaphoreType.DMA((6,)),
        ],
        out_shape=jax.ShapeDtypeStruct(chi.shape, F32),
        input_output_aliases={1 + len(flat_halos): 0},
        name="edge",
        compiler_params=pltpu.CompilerParams(vmem_limit_bytes=VMEM_LIMIT),
    )(edge, *flat_halos, chi)


def ring(low, high):
    count = lax.axis_size("row")
    up = [(i, (i + 1) % count) for i in range(count)]
    down = [(j, i) for i, j in up]
    return lax.ppermute(low, "row", up), lax.ppermute(high, "row", down)


def green_operands(green):
    mol_dev = green.shape[2]
    virtual = green[1].reshape(NTAU, mol_dev, NN, BO, BO)
    virtual = jnp.transpose(virtual, (1, 0, 3, 2, 4)).reshape(mol_dev, NTAU, BO, NN * BO)
    below, above = ring(virtual[mol_dev - HALF :], virtual[:HALF])
    occupied = green[0].reshape(NTAU, mol_dev, NN, BO, BO)
    first = occupied[:, :HALF]
    first = jnp.stack([first[:, :, 0], first[:, :, 1], first[:, :, 1]], axis=2)
    occupied = jnp.concatenate([first, occupied[:, :, HALF:]], axis=1)
    occupied = jnp.transpose(occupied, (1, 0, 2, 4, 3))
    return (below, virtual, above), occupied.reshape(mol_dev + HALF, NTAU, KEPT * BO, BO)


def shards(b3_store, block_shift, green, block_mask):
    devices = lax.axis_size("row")
    myself = lax.axis_index("row")
    mol_dev, _, aux, size = b3_store.shape
    count = mol_dev * NN
    capacity = (count + devices - 1) // devices
    pair = 2 if capacity > 1 else 1
    halves = (capacity + pair - 1) // pair
    shifts = block_shift.reshape(count)
    position = jnp.arange(count, dtype=jnp.int32)
    same = (shifts[:, None] == shifts[None, :]) & (position[None, :] < position[:, None])
    rank = jnp.sum(same.astype(jnp.int32), axis=1)
    target = (myself - shifts) % devices
    anchor = (myself + shifts) % devices
    store = b3_store.reshape(count, aux, size)
    mask = block_mask.reshape(count)
    chunks = chunk_groups(aux)
    widen = jnp.asarray(np.repeat(np.eye(BO, dtype=np.float32), 8, axis=1), BF)

    outgoing = [pack_blocks(store, target, rank, devices, capacity, groups) for groups in chunks]
    virtual, occupied = green_operands(green)
    arrived = lax.all_to_all(outgoing[0], "row", split_axis=0, concat_axis=0, tiled=True)
    arrived, virtual, occupied = lax.optimization_barrier((arrived, virtual, occupied))
    parts, folded, lows, highs = [], [], [], []
    for c, groups in enumerate(chunks):
        if c + 1 < len(chunks):
            arrived, sent, folded = lax.optimization_barrier((arrived, outgoing[c + 1], folded))
            coming = lax.all_to_all(sent, "row", split_axis=0, concat_axis=0, tiled=True)
        else:
            arrived, folded = lax.optimization_barrier((arrived, folded))
        own, first, last = spread_out(arrived, anchor, rank, mask, aux, capacity, groups)
        below, above = ring(last, first)
        parts.append(own)
        lows.append(below)
        highs.append(above)
        if c + 1 < len(chunks):
            folded = [*folded, fold_kernel(own, virtual, occupied, widen)]
            arrived = coming
    chi, edge = chi_kernel(parts, folded, virtual, occupied, widen, chunks, aux)
    chi = edge_kernel(chi, edge, (lows, highs), chunks, aux)
    return jnp.transpose(chi, (2, 0, 1, 3))


def solution(mesh):
    in_specs = (
        P(("groups", "row"), None, None, None),
        P("groups", None),
        P(None, None, ("groups", "row"), None, None),
        P(("groups", "row"), None),
    )
    out_specs = P(None, ("groups", "row"), None, None)
    return jax.shard_map(shards, mesh=mesh, in_specs=in_specs, out_specs=out_specs, check_vma=False)
```

time: 226 us -> 196 us (0.87)
  waiting for transfers between devices: 60.3 us -> 29 us
  Pallas kernels: 113 us -> 93.9 us
  local copies, waits for them, and re-layouts: 9.82 us -> 28.2 us
  starting transfers between devices: 38.4 us -> 40.7 us
    all_to_all x2, waiting for transfers between devices: 60.3 us -> 3.58 us  [the longest x1 3.27 us: shards(): lax.all_to_all(outgoing[0], 'row', split_axis=0, concat_axis=0, tiled=True)]
    ppermute x6, waiting for transfers between devices: 0.02 us -> 25.4 us  [ring(): return (lax.ppermute(low, 'row', up), lax.ppermute(high, 'row', down))]
    pallas_call x2 -> x1, Pallas kernels: 42.5 us -> 21.4 us  [fold_kernel(): call(body, 'fold', (units,), [pl.BlockSpec((1, *own.shape[1:]), lambda u:...]
    slice x2 -> x4, local copies, waits for them, and re-layouts: 0.08 us -> 6.03 us  [the longest x3 4.2 us: green_operands(): below, above = ring(virtual[mol_dev - HALF:], virtual[:HALF])]
    another operation x0 -> x2, local copies, waits for them, and re-layouts: none -> 3.92 us  [green_operands(): virtual = green[1].reshape(NTAU, mol_dev, NN, BO, BO)]
    unnamed x17 -> x19, local copies, waits for them, and re-layouts: 4.15 us -> 7.96 us
    pallas_call x3 -> x4, Pallas kernels: 56.1 us -> 59.1 us  [the longest x1 34.7 us: chi_kernel(): call(body, 'chi', (units + HALF,), [pl.BlockSpec(memory_space=pl.ANY)] *...]
    slice x2, local copies, waits for them, and re-layouts: 0.01 us -> 2.76 us  [green_operands(): first = jnp.stack([first[:, :, 0], first[:, :, 1], first[:, :, 1]], axis=2)]
  transfers between devices with their start and end apart: 8 -> 8, of which waited for: 1 -> 3; matrix products, arithmetic and copies ran while one was open for 4% -> 14% of each run, Pallas kernels for 36% -> 41%
where the time goes in v2:
time: 196 us; the launch traced here: 195 us
  Pallas kernels  93.9 us (48%)
  starting transfers between devices  40.7 us (21%)
  waiting for transfers between devices  29 us (15%)
  local copies, waits for them, and re-layouts  28.2 us (14%)
  other arithmetic  3.24 us (2%)
    pallas_call x1, Pallas kernels, chi_kernel(): call(body, 'chi', (units + HALF,), [pl.BlockSpec(memory_space=pl.ANY)] *...  34.7 us
    ppermute x6, waiting for transfers between devices, ring(): return (lax.ppermute(low, 'row', up), lax.ppermute(high, 'row', down))  25.4 us
    pallas_call x1, Pallas kernels, fold_kernel(): call(body, 'fold', (units,), [pl.BlockSpec((1, *own.shape[1:]), lambda u:...  21.4 us
    pallas_call x2, Pallas kernels, spread_out(): call(body, 'spread_out', (steps,), [pl.BlockSpec(incoming.shape, lambda a...  17.6 us
    all_to_all x1, starting transfers between devices, shards(): lax.all_to_all(sent, 'row', split_axis=0, concat_axis=0, tiled=True)  17.1 us
    ppermute x6, starting transfers between devices, ring(): return (lax.ppermute(low, 'row', up), lax.ppermute(high, 'row', down))  16.3 us
    pallas_call x2, Pallas kernels, pack_blocks(): call(body, 'pack_blocks', (steps,), [pl.BlockSpec((batch, 16, size), lamb...  13.3 us
    unnamed x19, local copies, waits for them, and re-layouts  7.96 us
  transfers between devices with their start and end apart: 8, of which 3 were waited for; matrix products, arithmetic and copies ran while one was open for 14% of the time, Pallas kernels for 41%

profile of v2, /device:TPU:0, one launch (start us, length us, event | category | flops | bytes accessed | tf_op | source)
XLA Modules:
  0.0 195.3 jit_solution(10063598849132453889)
XLA Ops:
  2.2 7.3 %pack_blocks.2 = bf16[16,96,1152]{2,1,0:T(8,128)(2,1)} custom-call(s32[60]{0:T(128)} %get-tuple-element.43.target_ref, s32[60]{0:T(128)} %convert_reduce_fusion.rank_ref, bf16[60,68,576]{2,1,0:T(8,128)(2,1)} %bitcast.12, bf16[60,68,576]{2,1,0:T(8,128)(2,1)} %bitcast.13, bf16[60,68,576]{2,1,0:T(8,128)(2,1)} %bitcast.14), custom_call_target="tpu_custom_call" | custom-call | tf_op jit(solution)/shard_map/pack_blocks/pallas_call | solution.py:86
  9.5 7.4 %all-to-all-start = ((bf16[16,96,1152]{2,1,0:T(8,128)(2,1)}), bf16[16,96,1152]{2,1,0:T(8,128)(2,1)S(1)}, u32[]{:S(2)}, u32[]{:S(2)}) async-start(bf16[16,96,1152]{2,1,0:T(8,128)(2,1)} %pack_blocks.2), calls=%async_computation | async-start | bytes 7077888 | tf_op jit(solution)/shard_map/all_to_all | solution.py:656
  16.9 1.9 fusion.4
  18.8 2.5 %reshape_squeeze.6 = bf16[2,12,5,24,24]{4,3,0,2,1:T(8,128)(2,1)} reshape(bf16[1,2,12,5,576]{4,1,3,2,0:T(2,128)(2,1)} %get-tuple-element.42) | data formatting | bytes 276480 | tf_op jit(solution)/shard_map/reshape;squeeze | solution.py:624
  24.5 1.7 slice.34
  26.6 1.7 slice.36
  28.3 4.0 %collective-permute-start.1 = (bf16[2,2,24,120]{3,2,1,0:T(8,128)(2,1)}, bf16[2,2,24,120]{3,2,1,0:T(8,128)(2,1)}, u32[]{:S(2)}, u32[]{:S(2)}) collective-permute-start(bf16[2,2,24,120]{3,2,1,0:T(8,128)(2,1)} %slice.36), channel_id=1, source_target_pairs={{1,0},{2,1},{3,2},{4,3},{5,4},{6,5},{7,6},{8,7},{9,8},{10,9},{11,1... | collective-permute-start | bytes 69128 | tf_op jit(solution)/shard_map/ppermute | solution.py:619
  32.4 2.5 %reshape_squeeze.7 = bf16[2,12,5,24,24]{4,3,0,2,1:T(8,128)(2,1)} reshape(bf16[1,2,12,5,576]{4,1,3,2,0:T(2,128)(2,1)} %get-tuple-element.41) | data formatting | bytes 276480 | tf_op jit(solution)/shard_map/reshape;squeeze | solution.py:627
  37.6 1.8 slice.45
  40.9 2.0 %copy.37 = bf16[2,12,3,24,24]{3,4,2,0,1:T(8,128)(2,1)} copy(bf16[2,12,3,24,24]{4,3,0,2,1:T(8,128)(2,1)} %slice.45) | data formatting | bytes 165888
  42.8 1.5 copy.35
  44.3 1.9 pad_maximum_fusion
  46.2 2.5 %reshape.22.mid_ref.refs_4_ = bf16[12,2,24,120]{3,2,1,0:T(8,128)(2,1)} reshape(bf16[12,2,24,5,24]{4,3,2,1,0:T(8,128)(2,1)} %bitcast.18) | data formatting | bytes 276480 | tf_op jit(solution)/shard_map/reshape | solution.py:625
  48.7 6.0 %pack_blocks.3 = bf16[16,40,1152]{2,1,0:T(8,128)(2,1)} custom-call(s32[60]{0:T(128)} %get-tuple-element.43.target_ref, s32[60]{0:T(128)} %convert_reduce_fusion.rank_ref, bf16[60,68,576]{2,1,0:T(8,128)(2,1)} %bitcast.15, bf16[60,68,576]{2,1,0:T(8,128)(2,1)} %bitcast.16), custom_call_target="tpu_custom_call" | custom-call | tf_op jit(solution)/shard_map/pack_blocks/pallas_call | solution.py:86
  54.7 25.4 %collective-permute-done.low_ref.refs_3_ = bf16[2,2,24,120]{3,2,1,0:T(8,128)(2,1)} collective-permute-done((bf16[2,2,24,120]{3,2,1,0:T(8,128)(2,1)}, bf16[2,2,24,120]{3,2,1,0:T(8,128)(2,1)}, u32[]{:S(2)}, u32[]{:S(2)}) %collective-permute-start) | collective-permute-done | bytes 23072 | tf_op jit(solution)/shard_map/ppermute | solution.py:619
  80.1 3.3 %all-to-all-done.in_ref = bf16[16,96,1152]{2,1,0:T(8,128)(2,1)S(1)} async-done(((bf16[16,96,1152]{2,1,0:T(8,128)(2,1)}), bf16[16,96,1152]{2,1,0:T(8,128)(2,1)S(1)}, u32[]{:S(2)}, u32[]{:S(2)}) %all-to-all-start) | async-done | bytes 3538976 | tf_op jit(solution)/shard_map/all_to_all | solution.py:656
  83.3 17.1 %all-to-all-start.1 = ((bf16[16,40,1152]{2,1,0:T(8,128)(2,1)}), bf16[16,40,1152]{2,1,0:T(8,128)(2,1)}, u32[]{:S(2)}, u32[]{:S(2)}) async-start(bf16[16,40,1152]{2,1,0:T(8,128)(2,1)} %pack_blocks.3), calls=%async_computation.1 | async-start | bytes 2949120 | tf_op jit(solution)/shard_map/all_to_all | solution.py:662
  101.1 9.8 %spread_out.2 = (bf16[12,48,3072]{2,1,0:T(8,128)(2,1)}, bf16[2,48,3072]{2,1,0:T(8,128)(2,1)}, bf16[2,48,3072]{2,1,0:T(8,128)(2,1)}) custom-call(s32[60]{0:T(128)} %get-tuple-element.44.source_ref, s32[60]{0:T(128)} %convert_reduce_fusion.rank_ref, s32[60]{0:T(128)} %reshape.20.mask_ref, bf16[16,96,1152]{2,1,0:T(8,128)(2,1)} %copy-done, ...), custom_call_target="tpu_custom_call" | custom-call | tf_op jit(solution)/shard_map/spread_out/pallas_call | solution.py:196
  111.3 4.1 %collective-permute-start.4 = (bf16[2,48,3072]{2,1,0:T(8,128)(2,1)}, bf16[2,48,3072]{2,1,0:T(8,128)(2,1)S(1)}, u32[]{:S(2)}, u32[]{:S(2)}) collective-permute-start(bf16[2,48,3072]{2,1,0:T(8,128)(2,1)} %get-tuple-element.36), channel_id=1, source_target_pairs={{1,0},{2,1},{3,2},{4,3},{5,4},{6,5},{7,6},{8,7},{9,8},{10,9},{11,1... | collective-permute-start | bytes 1769480 | tf_op jit(solution)/shard_map/ppermute | solution.py:619
  115.3 21.4 %fold.1.refs_2_ = bf16[14,3,96,3072]{3,2,1,0:T(8,128)(2,1)} custom-call(bf16[12,48,3072]{2,1,0:T(8,128)(2,1)} %get-tuple-element.24.own_ref.refs_0_, bf16[2,2,24,120]{3,2,1,0:T(8,128)(2,1)} %collective-permute-done.low_ref.refs_3_, bf16[12,2,24,120]{3,2,1,0:T(8,128)(2,1)} %reshape.22.mid_ref.refs_4_, ...), custom_call_target="tpu_custom_call" | custom-call | tf_op jit(solution)/shard_map/fold/pallas_call | solution.py:318
  137.1 7.8 %spread_out.3 = (bf16[12,32,3072]{2,1,0:T(8,128)(2,1)}, bf16[2,32,3072]{2,1,0:T(8,128)(2,1)}, bf16[2,32,3072]{2,1,0:T(8,128)(2,1)}) custom-call(s32[60]{0:T(128)} %get-tuple-element.44.source_ref, s32[60]{0:T(128)} %convert_reduce_fusion.rank_ref, s32[60]{0:T(128)} %reshape.20.mask_ref, bf16[16,40,1152]{2,1,0:T(8,128)(2,1)} %all-to-all-done.1.in_ref, ...), custom_call_target="tpu_custom_call" | custom-call | tf_op jit(solution)/shard_map/spread_out/pallas_call | solution.py:196
  145.7 6.7 %collective-permute-start.5 = (bf16[2,32,3072]{2,1,0:T(8,128)(2,1)}, bf16[2,32,3072]{2,1,0:T(8,128)(2,1)S(1)}, u32[]{:S(2)}, u32[]{:S(2)}) collective-permute-start(bf16[2,32,3072]{2,1,0:T(8,128)(2,1)} %get-tuple-element.37), channel_id=1, source_target_pairs={{1,0},{2,1},{3,2},{4,3},{5,4},{6,5},{7,6},{8,7},{9,8},{10,9},{11,1... | collective-permute-start | bytes 1179656 | tf_op jit(solution)/shard_map/ppermute | solution.py:619
  152.3 34.7 %chi.1 = (f32[12,5,2,4624]{3,2,1,0:T(2,128)}, bf16[6,160,3072]{2,1,0:T(8,128)(2,1)}) custom-call(bf16[12,48,3072]{2,1,0:T(8,128)(2,1)} %get-tuple-element.24.own_ref.refs_0_, bf16[12,32,3072]{2,1,0:T(8,128)(2,1)} %get-tuple-element.31.refs_1_, bf16[14,3,96,3072]{3,2,1,0:T(8,128)(2,1)} %fold.1.refs_2_, ...), custom_call_target="tpu_custom_call" | custom-call | tf_op jit(solution)/shard_map/chi/pallas_call | solution.py:519
  188.3 6.9 %edge.1 = f32[12,5,2,4624]{3,2,1,0:T(2,128)} custom-call(bf16[6,160,3072]{2,1,0:T(8,128)(2,1)} %get-tuple-element.33.edge_ref, bf16[2,48,3072]{2,1,0:T(8,128)(2,1)} %copy-done.2, bf16[2,32,3072]{2,1,0:T(8,128)(2,1)} %copy-done.4, bf16[2,48,3072]{2,1,0:T(8,128)(2,1)} %copy-done.3, bf16[2,32,3072]{2,1,0:T(8,128)(2,1)} %copy-done.5, ...), custom_call_target="tpu_custom_call", output_to_operand_aliasing={{}: (5, {})} | custom-call | tf_op jit(solution)/shard_map/edge/pallas_call | solution.py:594
  (34 shorter events, 13.4 us)
Async XLA Ops:
  9.5 73.8 %all-to-all-start = ((bf16[16,96,1152]{2,1,0:T(8,128)(2,1)}), bf16[16,96,1152]{2,1,0:T(8,128)(2,1)S(1)}, u32[]{:S(2)}, u32[]{:S(2)}) async-start(bf16[16,96,1152]{2,1,0:T(8,128)(2,1)} %pack_blocks.2), calls=%async_computation | async-start | bytes 7077888 | tf_op jit(solution)/shard_map/all_to_all | solution.py:656
  22.7 1.0 copy-start.1
  26.2 53.8 %collective-permute-start = (bf16[2,2,24,120]{3,2,1,0:T(8,128)(2,1)}, bf16[2,2,24,120]{3,2,1,0:T(8,128)(2,1)}, u32[]{:S(2)}, u32[]{:S(2)}) collective-permute-start(bf16[2,2,24,120]{3,2,1,0:T(8,128)(2,1)} %slice.34), channel_id=1, source_target_pairs={{0,1},{1,2},{2,3},{3,4},{4,5},{5,6},{6,7},{7,8},{8,9},{9,10},{10,1... | collective-permute-start | bytes 69128 | tf_op jit(solution)/shard_map/ppermute | solution.py:619
  28.3 51.7 %collective-permute-start.1 = (bf16[2,2,24,120]{3,2,1,0:T(8,128)(2,1)}, bf16[2,2,24,120]{3,2,1,0:T(8,128)(2,1)}, u32[]{:S(2)}, u32[]{:S(2)}) collective-permute-start(bf16[2,2,24,120]{3,2,1,0:T(8,128)(2,1)} %slice.36), channel_id=1, source_target_pairs={{1,0},{2,1},{3,2},{4,3},{5,4},{6,5},{7,6},{8,7},{9,8},{10,9},{11,1... | collective-permute-start | bytes 69128 | tf_op jit(solution)/shard_map/ppermute | solution.py:619
  54.7 45.7 %copy-start.6 = (s32[12,5]{0,1:T(8,128)S(1)}, s32[12,5]{0,1:T(8,128)}, u32[]{:S(2)}) copy-start(s32[12,5]{0,1:T(8,128)} %param.18) | copy-start | bytes 724
  83.3 17.8 %copy-start = (bf16[16,96,1152]{2,1,0:T(8,128)(2,1)}, bf16[16,96,1152]{2,1,0:T(8,128)(2,1)S(1)}, u32[]{:S(2)}) copy-start(bf16[16,96,1152]{2,1,0:T(8,128)(2,1)S(1)} %all-to-all-done.in_ref) | copy-start | bytes 10616836
  83.3 53.8 %all-to-all-start.1 = ((bf16[16,40,1152]{2,1,0:T(8,128)(2,1)}), bf16[16,40,1152]{2,1,0:T(8,128)(2,1)}, u32[]{:S(2)}, u32[]{:S(2)}) async-start(bf16[16,40,1152]{2,1,0:T(8,128)(2,1)} %pack_blocks.3), calls=%async_computation.1 | async-start | bytes 2949120 | tf_op jit(solution)/shard_map/all_to_all | solution.py:662
  110.9 76.1 %collective-permute-start.2 = (bf16[2,48,3072]{2,1,0:T(8,128)(2,1)}, bf16[2,48,3072]{2,1,0:T(8,128)(2,1)S(1)}, u32[]{:S(2)}, u32[]{:S(2)}) collective-permute-start(bf16[2,48,3072]{2,1,0:T(8,128)(2,1)} %get-tuple-element.34), channel_id=1, source_target_pairs={{0,1},{1,2},{2,3},{3,4},{4,5},{5,6},{6,7},{7,8},{8,9},{9,10},{10,1... | collective-permute-start | bytes 1769480 | tf_op jit(solution)/shard_map/ppermute | solution.py:619
  111.3 75.7 %collective-permute-start.4 = (bf16[2,48,3072]{2,1,0:T(8,128)(2,1)}, bf16[2,48,3072]{2,1,0:T(8,128)(2,1)S(1)}, u32[]{:S(2)}, u32[]{:S(2)}) collective-permute-start(bf16[2,48,3072]{2,1,0:T(8,128)(2,1)} %get-tuple-element.36), channel_id=1, source_target_pairs={{1,0},{2,1},{3,2},{4,3},{5,4},{6,5},{7,6},{8,7},{9,8},{10,9},{11,1... | collective-permute-start | bytes 1769480 | tf_op jit(solution)/shard_map/ppermute | solution.py:619
  144.9 42.2 %collective-permute-start.3 = (bf16[2,32,3072]{2,1,0:T(8,128)(2,1)}, bf16[2,32,3072]{2,1,0:T(8,128)(2,1)S(1)}, u32[]{:S(2)}, u32[]{:S(2)}) collective-permute-start(bf16[2,32,3072]{2,1,0:T(8,128)(2,1)} %get-tuple-element.35), channel_id=1, source_target_pairs={{0,1},{1,2},{2,3},{3,4},{4,5},{5,6},{6,7},{7,8},{8,9},{9,10},{10,1... | collective-permute-start | bytes 1179656 | tf_op jit(solution)/shard_map/ppermute | solution.py:619
  145.7 41.4 %collective-permute-start.5 = (bf16[2,32,3072]{2,1,0:T(8,128)(2,1)}, bf16[2,32,3072]{2,1,0:T(8,128)(2,1)S(1)}, u32[]{:S(2)}, u32[]{:S(2)}) collective-permute-start(bf16[2,32,3072]{2,1,0:T(8,128)(2,1)} %get-tuple-element.37), channel_id=1, source_target_pairs={{1,0},{2,1},{3,2},{4,3},{5,4},{6,5},{7,6},{8,7},{9,8},{10,9},{11,1... | collective-permute-start | bytes 1179656 | tf_op jit(solution)/shard_map/ppermute | solution.py:619
  187.0 0.8 copy-start.2
  187.0 1.0 copy-start.3
  187.0 1.1 copy-start.4
  187.0 1.2 copy-start.5

commit v3 on v2

--- a/solution.py
+++ b/solution.py
@@ -111,7 +111,7 @@
     return tables
 
 
-def spread_out(incoming, source, rank, mask, aux, capacity, groups):
+def spread_out(incoming, source, rank, mask, aux, capacity, groups, ends):
     size = BO * BO
     pair = 2 if capacity > 1 else 1
     halves = (capacity + pair - 1) // pair
@@ -124,10 +124,12 @@
     molecules = source.shape[0] // NN
     per_step = next(n for n in (6, 4, HALF) if molecules % n == 0)
     steps = molecules // per_step
+    held = ends[0].shape[1] if ends else 0
 
     def body(source_ref, rank_ref, mask_ref, in_ref, *refs):
         table_refs = refs[: len(tables)]
-        out_ref, first_ref, last_ref = refs[len(tables) :]
+        end_refs = refs[len(tables) : len(tables) + len(ends)]
+        out_ref, first_ref, last_ref = refs[len(tables) + len(ends) :]
         step = pl.program_id(0)
         lane = lax.broadcasted_iota(jnp.int32, (16, LANE), 1)
         stretches = [[] for _ in tables]
@@ -186,31 +188,37 @@
 
         @pl.when(step == 0)
         def _():
-            first_ref[...] = out_ref[:HALF]
+            if ends:
+                first_ref[:, :held] = end_refs[0][...]
+            first_ref[:, held:] = out_ref[:HALF]
 
         @pl.when(step == steps - 1)
         def _():
-            last_ref[...] = out_ref[per_step - HALF :]
+            if ends:
+                last_ref[:, :held] = end_refs[1][...]
+            last_ref[:, held:] = out_ref[per_step - HALF :]
 
     shape = (rows, BO * LANE)
+    end_shape = (HALF, held + rows, BO * LANE)
     return call(
         body,
         "spread_out",
         (steps,),
         [pl.BlockSpec(incoming.shape, lambda a, *_: (0, 0, 0))]
-        + [pl.BlockSpec(t.shape, lambda a, *_: (0, 0)) for _, _, t in tables],
+        + [pl.BlockSpec(t.shape, lambda a, *_: (0, 0)) for _, _, t in tables]
+        + [pl.BlockSpec(x.shape, lambda a, *_: (0, 0, 0)) for x in ends],
         [
             pl.BlockSpec((per_step, *shape), lambda a, *_: (a, 0, 0)),
-            pl.BlockSpec((HALF, *shape), lambda a, *_: (0, 0, 0)),
-            pl.BlockSpec((HALF, *shape), lambda a, *_: (0, 0, 0)),
+            pl.BlockSpec(end_shape, lambda a, *_: (0, 0, 0)),
+            pl.BlockSpec(end_shape, lambda a, *_: (0, 0, 0)),
         ],
         [
             jax.ShapeDtypeStruct((molecules, *shape), BF),
-            jax.ShapeDtypeStruct((HALF, *shape), BF),
-            jax.ShapeDtypeStruct((HALF, *shape), BF),
+            jax.ShapeDtypeStruct(end_shape, BF),
+            jax.ShapeDtypeStruct(end_shape, BF),
         ],
         prefetch=3,
-    )(source, rank, mask, incoming, *[jnp.asarray(t, BF) for _, _, t in tables])
+    )(source, rank, mask, incoming, *[jnp.asarray(t, BF) for _, _, t in tables], *ends)
 
 
 def place_windows(virtual_ref, a, slots, window_ref):
@@ -547,21 +555,20 @@
     )(*parts, *folded, *virtual, occupied, widen)
 
 
-def edge_kernel(chi, edge, halos, chunks, aux):
+def edge_kernel(chi, edge, below, above, chunks, aux):
     molecules = chi.shape[0]
     heights, _, plan = row_plan(chunks)
     rows = sum(heights)
     place = np.array([[0, 0, 1, molecules - 2, molecules - 1, molecules - 1], [0, 1, 0, 4, 3, 4]], np.int32)
     spots = sorted((g, c, at) for c, groups in enumerate(chunks) for at, g in enumerate(groups))
-    flat_halos = [h for side in halos for h in side]
-
-    def body(edge_ref, *refs):
-        below_refs, above_refs = refs[: len(chunks)], refs[len(chunks) : 2 * len(chunks)]
-        out_ref, all_ref, flat_ref, sem = refs[2 * len(chunks) + 1 :]
+    starts = [sum(heights[:c]) for c in range(len(chunks))]
+
+    def body(edge_ref, below_ref, above_ref, chi_ref, out_ref, all_ref, flat_ref, sem):
         e = pl.program_id(0)
 
         def take(side, i):
-            near = jnp.concatenate([side[c][i, at * 16 : (at + 1) * 16] for _, c, at in spots], axis=0)
+            tiles = [starts[c] + at * 16 for _, c, at in spots]
+            near = jnp.concatenate([side[i, at : at + 16] for at in tiles], axis=0)
             result = lax.dot_general(
                 edge_ref[0], near, (((1,), (1,)), ((), ())), preferred_element_type=F32
             )
@@ -570,11 +577,11 @@
 
         @pl.when(e < 3)
         def _():
-            take(below_refs, jnp.minimum(e, 1))
+            take(below_ref, jnp.minimum(e, 1))
 
         @pl.when(e >= 3)
         def _():
-            take(above_refs, jnp.maximum(e - 4, 0))
+            take(above_ref, jnp.maximum(e - 4, 0))
 
         @pl.when(e == 5)
         def _():
@@ -596,7 +603,8 @@
         grid=(6,),
         in_specs=[
             pl.BlockSpec((1, *edge.shape[1:]), lambda e: (e, 0, 0)),
-            *[pl.BlockSpec(h.shape, lambda e: (0, 0, 0)) for h in flat_halos],
+            pl.BlockSpec(below.shape, lambda e: (0, 0, 0)),
+            pl.BlockSpec(above.shape, lambda e: (0, 0, 0)),
             pl.BlockSpec(memory_space=pl.ANY),
         ],
         out_specs=pl.BlockSpec(memory_space=pl.ANY),
@@ -606,10 +614,10 @@
             pltpu.SemaphoreType.DMA((6,)),
         ],
         out_shape=jax.ShapeDtypeStruct(chi.shape, F32),
-        input_output_aliases={1 + len(flat_halos): 0},
+        input_output_aliases={3: 0},
         name="edge",
         compiler_params=pltpu.CompilerParams(vmem_limit_bytes=VMEM_LIMIT),
-    )(edge, *flat_halos, chi)
+    )(edge, below, above, chi)
 
 
 def ring(low, high):
@@ -655,23 +663,21 @@
     virtual, occupied = green_operands(green)
     arrived = lax.all_to_all(outgoing[0], "row", split_axis=0, concat_axis=0, tiled=True)
     arrived, virtual, occupied = lax.optimization_barrier((arrived, virtual, occupied))
-    parts, folded, lows, highs = [], [], [], []
+    parts, folded, ends = [], [], []
     for c, groups in enumerate(chunks):
         if c + 1 < len(chunks):
             arrived, sent, folded = lax.optimization_barrier((arrived, outgoing[c + 1], folded))
             coming = lax.all_to_all(sent, "row", split_axis=0, concat_axis=0, tiled=True)
         else:
             arrived, folded = lax.optimization_barrier((arrived, folded))
-        own, first, last = spread_out(arrived, anchor, rank, mask, aux, capacity, groups)
-        below, above = ring(last, first)
+        own, *ends = spread_out(arrived, anchor, rank, mask, aux, capacity, groups, ends)
         parts.append(own)
-        lows.append(below)
-        highs.append(above)
         if c + 1 < len(chunks):
             folded = [*folded, fold_kernel(own, virtual, occupied, widen)]
             arrived = coming
+    below, above = ring(ends[1], ends[0])
     chi, edge = chi_kernel(parts, folded, virtual, occupied, widen, chunks, aux)
-    chi = edge_kernel(chi, edge, (lows, highs), chunks, aux)
+    chi = edge_kernel(chi, edge, below, above, chunks, aux)
     return jnp.transpose(chi, (2, 0, 1, 3))
 
 

time: 196 us -> 191 us (0.974)
  starting transfers between devices: 40.7 us -> 34.7 us
    ppermute x6 -> x4, starting transfers between devices: 16.3 us -> 10.3 us  [ring(): return (lax.ppermute(low, 'row', up), lax.ppermute(high, 'row', down))]
    unnamed x19 -> x15, local copies, waits for them, and re-layouts: 7.96 us -> 8.02 us
    ppermute x6 -> x4, waiting for transfers between devices: 25.4 us -> 25.4 us  [ring(): return (lax.ppermute(low, 'row', up), lax.ppermute(high, 'row', down))]
  transfers between devices with their start and end apart: 8 -> 6, of which waited for: 3 -> 2; matrix products, arithmetic and copies ran while one was open for 14% -> 14% of each run, Pallas kernels for 41% -> 38%
where the time goes in v3:
time: 191 us; the launch traced here: 190 us
  Pallas kernels  94.6 us (50%)
  starting transfers between devices  34.7 us (18%)
  waiting for transfers between devices  28.7 us (15%)
  local copies, waits for them, and re-layouts  28.3 us (15%)
  other arithmetic  3.22 us (2%)
    pallas_call x1, Pallas kernels, chi_kernel(): call(body, 'chi', (units + HALF,), [pl.BlockSpec(memory_space=pl.ANY)] *...  34.6 us
    ppermute x4, waiting for transfers between devices, ring(): return (lax.ppermute(low, 'row', up), lax.ppermute(high, 'row', down))  25.4 us
    pallas_call x1, Pallas kernels, fold_kernel(): call(body, 'fold', (units,), [pl.BlockSpec((1, *own.shape[1:]), lambda u:...  21.5 us
    pallas_call x2, Pallas kernels, spread_out(): call(body, 'spread_out', (steps,), [pl.BlockSpec(incoming.shape, lambda a...  18.4 us
    all_to_all x1, starting transfers between devices, shards(): lax.all_to_all(sent, 'row', split_axis=0, concat_axis=0, tiled=True)  17.1 us
    pallas_call x2, Pallas kernels, pack_blocks(): call(body, 'pack_blocks', (steps,), [pl.BlockSpec((batch, 16, size), lamb...  13.2 us
    ppermute x4, starting transfers between devices, ring(): return (lax.ppermute(low, 'row', up), lax.ppermute(high, 'row', down))  10.3 us
    unnamed x15, local copies, waits for them, and re-layouts  8.02 us
  transfers between devices with their start and end apart: 6, of which 2 were waited for; matrix products, arithmetic and copies ran while one was open for 14% of the time, Pallas kernels for 38%

profile of v3, /device:TPU:0, one launch (start us, length us, event | category | flops | bytes accessed | tf_op | source)
XLA Modules:
  0.0 189.9 jit_solution(17963612739928824842)
XLA Ops:
  2.2 7.3 %pack_blocks.2 = bf16[16,96,1152]{2,1,0:T(8,128)(2,1)} custom-call(s32[60]{0:T(128)} %get-tuple-element.43.target_ref, s32[60]{0:T(128)} %convert_reduce_fusion.rank_ref, bf16[60,68,576]{2,1,0:T(8,128)(2,1)} %bitcast.12, bf16[60,68,576]{2,1,0:T(8,128)(2,1)} %bitcast.13, bf16[60,68,576]{2,1,0:T(8,128)(2,1)} %bitcast.14), custom_call_target="tpu_custom_call" | custom-call | tf_op jit(solution)/shard_map/pack_blocks/pallas_call | solution.py:86
  9.5 7.4 %all-to-all-start = ((bf16[16,96,1152]{2,1,0:T(8,128)(2,1)}), bf16[16,96,1152]{2,1,0:T(8,128)(2,1)S(1)}, u32[]{:S(2)}, u32[]{:S(2)}) async-start(bf16[16,96,1152]{2,1,0:T(8,128)(2,1)} %pack_blocks.2), calls=%async_computation | async-start | bytes 7077888 | tf_op jit(solution)/shard_map/all_to_all | solution.py:664
  16.9 1.9 %fusion.4 = (bf16[1,2,12,5,576]{4,1,3,2,0:T(2,128)(2,1)}, bf16[1,2,12,5,576]{4,1,3,2,0:T(2,128)(2,1)}) fusion(bf16[2,2,12,5,576]{4,1,3,2,0:T(2,128)(2,1)} %param.17), kind=kLoop, calls=%fused_computation.14 | loop fusion | bytes 552960 | tf_op jit(solution)/shard_map/slice | solution.py:635
  18.8 2.5 %reshape_squeeze.6 = bf16[2,12,5,24,24]{4,3,0,2,1:T(8,128)(2,1)} reshape(bf16[1,2,12,5,576]{4,1,3,2,0:T(2,128)(2,1)} %get-tuple-element.42) | data formatting | bytes 276480 | tf_op jit(solution)/shard_map/reshape;squeeze | solution.py:632
  21.3 1.4 copy.39
  24.6 1.7 slice.34
  26.6 1.7 slice.36
  28.3 4.0 %collective-permute-start.1 = (bf16[2,2,24,120]{3,2,1,0:T(8,128)(2,1)}, bf16[2,2,24,120]{3,2,1,0:T(8,128)(2,1)}, u32[]{:S(2)}, u32[]{:S(2)}) collective-permute-start(bf16[2,2,24,120]{3,2,1,0:T(8,128)(2,1)} %slice.36), channel_id=1, source_target_pairs={{1,0},{2,1},{3,2},{4,3},{5,4},{6,5},{7,6},{8,7},{9,8},{10,9},{11,1... | collective-permute-start | bytes 69128 | tf_op jit(solution)/shard_map/ppermute | solution.py:627
  32.4 2.5 %reshape_squeeze.7 = bf16[2,12,5,24,24]{4,3,0,2,1:T(8,128)(2,1)} reshape(bf16[1,2,12,5,576]{4,1,3,2,0:T(2,128)(2,1)} %get-tuple-element.41) | data formatting | bytes 276480 | tf_op jit(solution)/shard_map/reshape;squeeze | solution.py:635
  37.6 1.8 slice.45
  40.9 2.0 %copy.37 = bf16[2,12,3,24,24]{3,4,2,0,1:T(8,128)(2,1)} copy(bf16[2,12,3,24,24]{4,3,0,2,1:T(8,128)(2,1)} %slice.45) | data formatting | bytes 165888
  42.8 1.5 copy.35
  44.3 1.9 %pad_maximum_fusion = bf16[2,14,3,24,24]{3,4,2,0,1:T(8,128)(2,1)} fusion(bf16[2,12,3,24,24]{3,4,2,0,1:T(8,128)(2,1)} %copy.37, bf16[2,2,1,24,24]{3,4,2,0,1:T(8,128)(2,1)} %copy.36, bf16[2,2,2,24,24]{3,4,2,0,1:T(8,128)(2,1)} %copy.35), kind=kLoop, calls=%fused_computation.1 | loop fusion | flops 96768 | bytes 193536 | tf_op jit(solution)/shard_map/concatenate | solution.py:638
  46.2 2.5 %reshape.22.mid_ref.refs_4_ = bf16[12,2,24,120]{3,2,1,0:T(8,128)(2,1)} reshape(bf16[12,2,24,5,24]{4,3,2,1,0:T(8,128)(2,1)} %bitcast.18) | data formatting | bytes 276480 | tf_op jit(solution)/shard_map/reshape | solution.py:633
  48.7 5.9 %pack_blocks.3 = bf16[16,40,1152]{2,1,0:T(8,128)(2,1)} custom-call(s32[60]{0:T(128)} %get-tuple-element.43.target_ref, s32[60]{0:T(128)} %convert_reduce_fusion.rank_ref, bf16[60,68,576]{2,1,0:T(8,128)(2,1)} %bitcast.15, bf16[60,68,576]{2,1,0:T(8,128)(2,1)} %bitcast.16), custom_call_target="tpu_custom_call" | custom-call | tf_op jit(solution)/shard_map/pack_blocks/pallas_call | solution.py:86
  54.6 25.4 %collective-permute-done.low_ref.refs_3_ = bf16[2,2,24,120]{3,2,1,0:T(8,128)(2,1)} collective-permute-done((bf16[2,2,24,120]{3,2,1,0:T(8,128)(2,1)}, bf16[2,2,24,120]{3,2,1,0:T(8,128)(2,1)}, u32[]{:S(2)}, u32[]{:S(2)}) %collective-permute-start) | collective-permute-done | bytes 23072 | tf_op jit(solution)/shard_map/ppermute | solution.py:627
  80.1 3.3 %all-to-all-done.in_ref = bf16[16,96,1152]{2,1,0:T(8,128)(2,1)S(1)} async-done(((bf16[16,96,1152]{2,1,0:T(8,128)(2,1)}), bf16[16,96,1152]{2,1,0:T(8,128)(2,1)S(1)}, u32[]{:S(2)}, u32[]{:S(2)}) %all-to-all-start) | async-done | bytes 3538976 | tf_op jit(solution)/shard_map/all_to_all | solution.py:664
  83.3 17.1 %all-to-all-start.1 = ((bf16[16,40,1152]{2,1,0:T(8,128)(2,1)}), bf16[16,40,1152]{2,1,0:T(8,128)(2,1)}, u32[]{:S(2)}, u32[]{:S(2)}) async-start(bf16[16,40,1152]{2,1,0:T(8,128)(2,1)} %pack_blocks.3), calls=%async_computation.1 | async-start | bytes 2949120 | tf_op jit(solution)/shard_map/all_to_all | solution.py:670
  101.1 9.8 %spread_out.2 = (bf16[12,48,3072]{2,1,0:T(8,128)(2,1)}, bf16[2,48,3072]{2,1,0:T(8,128)(2,1)}, bf16[2,48,3072]{2,1,0:T(8,128)(2,1)}) custom-call(s32[60]{0:T(128)} %get-tuple-element.44.source_ref, s32[60]{0:T(128)} %convert_reduce_fusion.rank_ref, s32[60]{0:T(128)} %reshape.20.mask_ref, bf16[16,96,1152]{2,1,0:T(8,128)(2,1)} %copy-done, ...), custom_call_target="tpu_custom_call" | custom-call | tf_op jit(solution)/shard_map/spread_out/pallas_call | solution.py:203
  110.9 21.5 %fold.1.refs_2_ = bf16[14,3,96,3072]{3,2,1,0:T(8,128)(2,1)} custom-call(bf16[12,48,3072]{2,1,0:T(8,128)(2,1)} %get-tuple-element.24.own_ref.refs_0_, bf16[2,2,24,120]{3,2,1,0:T(8,128)(2,1)} %collective-permute-done.low_ref.refs_3_, bf16[12,2,24,120]{3,2,1,0:T(8,128)(2,1)} %reshape.22.mid_ref.refs_4_, ...), custom_call_target="tpu_custom_call" | custom-call | tf_op jit(solution)/shard_map/fold/pallas_call | solution.py:326
  132.3 8.6 %spread_out.3 = (bf16[12,32,3072]{2,1,0:T(8,128)(2,1)}, bf16[2,80,3072]{2,1,0:T(8,128)(2,1)}, bf16[2,80,3072]{2,1,0:T(8,128)(2,1)}) custom-call(s32[60]{0:T(128)} %get-tuple-element.44.source_ref, s32[60]{0:T(128)} %convert_reduce_fusion.rank_ref, s32[60]{0:T(128)} %reshape.20.mask_ref, bf16[16,40,1152]{2,1,0:T(8,128)(2,1)} %all-to-all-done.1.in_ref, ...), custom_call_target="tpu_custom_call" | custom-call | tf_op jit(solution)/shard_map/spread_out/pallas_call | solution.py:203
  141.3 5.5 %collective-permute-start.3 = (bf16[2,80,3072]{2,1,0:T(8,128)(2,1)}, bf16[2,80,3072]{2,1,0:T(8,128)(2,1)S(1)}, u32[]{:S(2)}, u32[]{:S(2)}) collective-permute-start(bf16[2,80,3072]{2,1,0:T(8,128)(2,1)} %get-tuple-element.37), channel_id=1, source_target_pairs={{1,0},{2,1},{3,2},{4,3},{5,4},{6,5},{7,6},{8,7},{9,8},{10,9},{11,1... | collective-permute-start | bytes 2949128 | tf_op jit(solution)/shard_map/ppermute | solution.py:627
  146.8 34.6 %chi.1 = (f32[12,5,2,4624]{3,2,1,0:T(2,128)}, bf16[6,160,3072]{2,1,0:T(8,128)(2,1)}) custom-call(bf16[12,48,3072]{2,1,0:T(8,128)(2,1)} %get-tuple-element.24.own_ref.refs_0_, bf16[12,32,3072]{2,1,0:T(8,128)(2,1)} %get-tuple-element.33.refs_1_, bf16[14,3,96,3072]{3,2,1,0:T(8,128)(2,1)} %fold.1.refs_2_, ...), custom_call_target="tpu_custom_call" | custom-call | tf_op jit(solution)/shard_map/chi/pallas_call | solution.py:527
  182.8 6.9 %edge.1 = f32[12,5,2,4624]{3,2,1,0:T(2,128)} custom-call(bf16[6,160,3072]{2,1,0:T(8,128)(2,1)} %get-tuple-element.35.edge_ref, bf16[2,80,3072]{2,1,0:T(8,128)(2,1)} %copy-done.2, bf16[2,80,3072]{2,1,0:T(8,128)(2,1)} %copy-done.3, f32[12,5,2,4624]{3,2,1,0:T(2,128)} %get-tuple-element.38.chi_ref), custom_call_target="tpu_custom_call", output_to_operand_aliasing={{}: (3, {})} | custom-call | tf_op jit(solution)/shard_map/edge/pallas_call | solution.py:601
  (26 shorter events, 10.9 us)
Async XLA Ops:
  9.5 73.8 %all-to-all-start = ((bf16[16,96,1152]{2,1,0:T(8,128)(2,1)}), bf16[16,96,1152]{2,1,0:T(8,128)(2,1)S(1)}, u32[]{:S(2)}, u32[]{:S(2)}) async-start(bf16[16,96,1152]{2,1,0:T(8,128)(2,1)} %pack_blocks.2), calls=%async_computation | async-start | bytes 7077888 | tf_op jit(solution)/shard_map/all_to_all | solution.py:664
  22.7 1.0 copy-start.1
  26.2 53.8 %collective-permute-start = (bf16[2,2,24,120]{3,2,1,0:T(8,128)(2,1)}, bf16[2,2,24,120]{3,2,1,0:T(8,128)(2,1)}, u32[]{:S(2)}, u32[]{:S(2)}) collective-permute-start(bf16[2,2,24,120]{3,2,1,0:T(8,128)(2,1)} %slice.34), channel_id=1, source_target_pairs={{0,1},{1,2},{2,3},{3,4},{4,5},{5,6},{6,7},{7,8},{8,9},{9,10},{10,1... | collective-permute-start | bytes 69128 | tf_op jit(solution)/shard_map/ppermute | solution.py:627
  28.3 51.7 %collective-permute-start.1 = (bf16[2,2,24,120]{3,2,1,0:T(8,128)(2,1)}, bf16[2,2,24,120]{3,2,1,0:T(8,128)(2,1)}, u32[]{:S(2)}, u32[]{:S(2)}) collective-permute-start(bf16[2,2,24,120]{3,2,1,0:T(8,128)(2,1)} %slice.36), channel_id=1, source_target_pairs={{1,0},{2,1},{3,2},{4,3},{5,4},{6,5},{7,6},{8,7},{9,8},{10,9},{11,1... | collective-permute-start | bytes 69128 | tf_op jit(solution)/shard_map/ppermute | solution.py:627
  54.6 45.8 %copy-start.4 = (s32[12,5]{0,1:T(8,128)S(1)}, s32[12,5]{0,1:T(8,128)}, u32[]{:S(2)}) copy-start(s32[12,5]{0,1:T(8,128)} %param.18) | copy-start | bytes 724
  83.3 17.8 %copy-start = (bf16[16,96,1152]{2,1,0:T(8,128)(2,1)}, bf16[16,96,1152]{2,1,0:T(8,128)(2,1)S(1)}, u32[]{:S(2)}) copy-start(bf16[16,96,1152]{2,1,0:T(8,128)(2,1)S(1)} %all-to-all-done.in_ref) | copy-start | bytes 10616836
  83.3 49.0 %all-to-all-start.1 = ((bf16[16,40,1152]{2,1,0:T(8,128)(2,1)}), bf16[16,40,1152]{2,1,0:T(8,128)(2,1)}, u32[]{:S(2)}, u32[]{:S(2)}) async-start(bf16[16,40,1152]{2,1,0:T(8,128)(2,1)} %pack_blocks.3), calls=%async_computation.1 | async-start | bytes 2949120 | tf_op jit(solution)/shard_map/all_to_all | solution.py:670
  140.9 40.5 %collective-permute-start.2 = (bf16[2,80,3072]{2,1,0:T(8,128)(2,1)}, bf16[2,80,3072]{2,1,0:T(8,128)(2,1)S(1)}, u32[]{:S(2)}, u32[]{:S(2)}) collective-permute-start(bf16[2,80,3072]{2,1,0:T(8,128)(2,1)} %get-tuple-element.36), channel_id=1, source_target_pairs={{0,1},{1,2},{2,3},{3,4},{4,5},{5,6},{6,7},{7,8},{8,9},{9,10},{10,1... | collective-permute-start | bytes 2949128 | tf_op jit(solution)/shard_map/ppermute | solution.py:627
  141.3 40.2 %collective-permute-start.3 = (bf16[2,80,3072]{2,1,0:T(8,128)(2,1)}, bf16[2,80,3072]{2,1,0:T(8,128)(2,1)S(1)}, u32[]{:S(2)}, u32[]{:S(2)}) collective-permute-start(bf16[2,80,3072]{2,1,0:T(8,128)(2,1)} %get-tuple-element.37), channel_id=1, source_target_pairs={{1,0},{2,1},{3,2},{4,3},{5,4},{6,5},{7,6},{8,7},{9,8},{10,9},{11,1... | collective-permute-start | bytes 2949128 | tf_op jit(solution)/shard_map/ppermute | solution.py:627
  181.5 0.9 copy-start.2
  181.5 1.3 copy-start.3

commit v4 on v3

--- a/solution.py
+++ b/solution.py
@@ -17,7 +17,8 @@
 KEPT = 3
 BF = jnp.bfloat16
 F32 = jnp.float32
-VMEM_LIMIT = 56 * 1024 * 1024
+MIB = 1024 * 1024
+VMEM = {"pack_blocks": 56, "spread_out": 30, "fold": 44, "chi": 46, "edge": 16}
 
 
 def call(body, name, grid, in_specs, out_specs, out_shape, scratch=(), prefetch=0):
@@ -32,7 +33,7 @@
         ),
         out_shape=out_shape,
         name=name,
-        compiler_params=pltpu.CompilerParams(vmem_limit_bytes=VMEM_LIMIT),
+        compiler_params=pltpu.CompilerParams(vmem_limit_bytes=VMEM[name] * MIB),
     )
 
 
@@ -616,7 +617,7 @@
         out_shape=jax.ShapeDtypeStruct(chi.shape, F32),
         input_output_aliases={3: 0},
         name="edge",
-        compiler_params=pltpu.CompilerParams(vmem_limit_bytes=VMEM_LIMIT),
+        compiler_params=pltpu.CompilerParams(vmem_limit_bytes=VMEM["edge"] * MIB),
     )(edge, below, above, chi)
 
 

time: 191 us -> 186 us (0.974)
  waiting for transfers between devices: 28.7 us -> 51.7 us
  Pallas kernels: 94.6 us -> 80.3 us
  local copies, waits for them, and re-layouts: 28.3 us -> 18.1 us
    ppermute x4, waiting for transfers between devices: 25.4 us -> 48.2 us  [ring(): return (lax.ppermute(low, 'row', up), lax.ppermute(high, 'row', down))]
    pallas_call x2, Pallas kernels: 18.4 us -> 10.6 us  [spread_out(): call(body, 'spread_out', (steps,), [pl.BlockSpec(incoming.shape, lambda a...]
    unnamed x15 -> x43, local copies, waits for them, and re-layouts: 8.02 us -> 14.4 us
    slice x3, local copies, waits for them, and re-layouts: 4.2 us -> 0.35 us  [green_operands(): below, above = ring(virtual[mol_dev - HALF:], virtual[:HALF])]
    pallas_call x1, Pallas kernels: 6.93 us -> 3.41 us  [edge_kernel(): pl.pallas_call(body, grid=(6,), in_specs=[pl.BlockSpec((1, *edge.shape[1:...]
    another operation x2, local copies, waits for them, and re-layouts: 3.92 us -> 1.02 us  [green_operands(): virtual = green[1].reshape(NTAU, mol_dev, NN, BO, BO)]
    slice x2, local copies, waits for them, and re-layouts: 2.76 us -> 0.01 us  [green_operands(): first = jnp.stack([first[:, :, 0], first[:, :, 1], first[:, :, 1]], axis=2)]
    pallas_call x1, Pallas kernels: 34.6 us -> 32.5 us  [chi_kernel(): call(body, 'chi', (units + HALF,), [pl.BlockSpec(memory_space=pl.ANY)] *...]
  transfers between devices with their start and end apart: 6 -> 6, of which waited for: 2 -> 2; matrix products, arithmetic and copies ran while one was open for 14% -> 2% of each run, Pallas kernels for 38% -> 35%
where the time goes in v4:
time: 186 us
  Pallas kernels  80.3 us (43%)
  waiting for transfers between devices  51.7 us (28%)
  starting transfers between devices  33.8 us (18%)
  local copies, waits for them, and re-layouts  18.1 us (10%)
    ppermute x4, waiting for transfers between devices, ring(): return (lax.ppermute(low, 'row', up), lax.ppermute(high, 'row', down))  48.2 us
    pallas_call x1, Pallas kernels, chi_kernel(): call(body, 'chi', (units + HALF,), [pl.BlockSpec(memory_space=pl.ANY)] *...  32.5 us
    pallas_call x1, Pallas kernels, fold_kernel(): call(body, 'fold', (units,), [pl.BlockSpec((1, *own.shape[1:]), lambda u:...  20.1 us
    all_to_all x1, starting transfers between devices, shards(): lax.all_to_all(sent, 'row', split_axis=0, concat_axis=0, tiled=True)  17 us
    unnamed x43, local copies, waits for them, and re-layouts  14.4 us
    pallas_call x2, Pallas kernels, pack_blocks(): call(body, 'pack_blocks', (steps,), [pl.BlockSpec((batch, 16, size), lamb...  13.6 us
    pallas_call x2, Pallas kernels, spread_out(): call(body, 'spread_out', (steps,), [pl.BlockSpec(incoming.shape, lambda a...  10.6 us
    ppermute x4, starting transfers between devices, ring(): return (lax.ppermute(low, 'row', up), lax.ppermute(high, 'row', down))  9.28 us
  transfers between devices with their start and end apart: 6, of which 2 were waited for; matrix products, arithmetic and copies ran while one was open for 2% of the time, Pallas kernels for 35%

profile of v4, /device:TPU:0, one launch (start us, length us, event | category | flops | bytes accessed | tf_op | source)
XLA Modules:
  0.0 185.6 jit_solution(7257608574502820329)
XLA Ops:
  2.1 7.5 %pack_blocks.2 = bf16[16,96,1152]{2,1,0:T(8,128)(2,1)} custom-call(s32[60]{0:T(128)} %get-tuple-element.43.target_ref, s32[60]{0:T(128)} %convert_reduce_fusion.rank_ref, bf16[60,68,576]{2,1,0:T(8,128)(2,1)} %bitcast.14, bf16[60,68,576]{2,1,0:T(8,128)(2,1)} %bitcast.15, bf16[60,68,576]{2,1,0:T(8,128)(2,1)} %bitcast.16), custom_call_target="tpu_custom_call" | custom-call | tf_op jit(solution)/shard_map/pack_blocks/pallas_call | solution.py:87
  9.6 7.5 %all-to-all-start = ((bf16[16,96,1152]{2,1,0:T(8,128)(2,1)}), bf16[16,96,1152]{2,1,0:T(8,128)(2,1)}, u32[]{:S(2)}, u32[]{:S(2)}) async-start(bf16[16,96,1152]{2,1,0:T(8,128)(2,1)} %pack_blocks.2), calls=%async_computation | async-start | bytes 7077888 | tf_op jit(solution)/shard_map/all_to_all | solution.py:665
  19.2 4.1 %collective-permute-start.1 = (bf16[2,2,24,120]{3,2,1,0:T(8,128)(2,1)S(1)}, bf16[2,2,24,120]{3,2,1,0:T(8,128)(2,1)S(1)}, u32[]{:S(2)}, u32[]{:S(2)}) collective-permute-start(bf16[2,2,24,120]{3,2,1,0:T(8,128)(2,1)S(1)} %slice.36), channel_id=1, source_target_pairs={{1,0},{2,1},{3,2},{4,3},{5,4},{6,5},{7,6},{8,7},{9,8},{10,9},{11,1... | collective-permute-start | bytes 69128 | tf_op jit(solution)/shard_map/ppermute | solution.py:628
  24.6 1.2 reshape.22.mid_ref.refs_4_
  25.9 6.1 %pack_blocks.3 = bf16[16,40,1152]{2,1,0:T(8,128)(2,1)} custom-call(s32[60]{0:T(128)} %get-tuple-element.43.target_ref, s32[60]{0:T(128)} %convert_reduce_fusion.rank_ref, bf16[60,68,576]{2,1,0:T(8,128)(2,1)} %bitcast.17, bf16[60,68,576]{2,1,0:T(8,128)(2,1)} %bitcast.18), custom_call_target="tpu_custom_call" | custom-call | tf_op jit(solution)/shard_map/pack_blocks/pallas_call | solution.py:87
  32.0 48.2 %collective-permute-done.low_ref.refs_3_ = bf16[2,2,24,120]{3,2,1,0:T(8,128)(2,1)S(1)} collective-permute-done((bf16[2,2,24,120]{3,2,1,0:T(8,128)(2,1)S(1)}, bf16[2,2,24,120]{3,2,1,0:T(8,128)(2,1)S(1)}, u32[]{:S(2)}, u32[]{:S(2)}) %collective-permute-start) | collective-permute-done | bytes 23072 | tf_op jit(solution)/shard_map/ppermute | solution.py:628
  80.2 3.5 %all-to-all-done.in_ref = bf16[16,96,1152]{2,1,0:T(8,128)(2,1)} async-done(((bf16[16,96,1152]{2,1,0:T(8,128)(2,1)}), bf16[16,96,1152]{2,1,0:T(8,128)(2,1)}, u32[]{:S(2)}, u32[]{:S(2)}) %all-to-all-start) | async-done | bytes 3538976 | tf_op jit(solution)/shard_map/all_to_all | solution.py:665
  83.7 17.0 %all-to-all-start.1 = ((bf16[16,40,1152]{2,1,0:T(8,128)(2,1)}), bf16[16,40,1152]{2,1,0:T(8,128)(2,1)S(1)}, u32[]{:S(2)}, u32[]{:S(2)}) async-start(bf16[16,40,1152]{2,1,0:T(8,128)(2,1)} %pack_blocks.3), calls=%async_computation.1 | async-start | bytes 2949120 | tf_op jit(solution)/shard_map/all_to_all | solution.py:671
  100.9 1.2 copy-done.4
  102.1 1.2 copy-done.6
  103.3 6.8 %spread_out.2 = (bf16[12,48,3072]{2,1,0:T(8,128)(2,1)S(1)}, bf16[2,48,3072]{2,1,0:T(8,128)(2,1)S(1)}, bf16[2,48,3072]{2,1,0:T(8,128)(2,1)S(1)}) custom-call(s32[60]{0:T(128)S(1)} %get-tuple-element.44.source_ref, s32[60]{0:T(128)S(1)} %copy-done.16, s32[60]{0:T(128)S(1)} %reshape.20.mask_ref, bf16[16,96,1152]{2,1,0:T(8,128)(2,1)} %all-to-all-done.in_ref, ...), custom_call_target="tpu_custom_call" | custom-call | tf_op jit(solution)/shard_map/spread_out/pallas_call | solution.py:204
  110.2 0.8 copy-done.11
  111.0 0.8 copy-done.13
  111.8 20.1 %fold.1.refs_2_ = bf16[14,3,96,3072]{3,2,1,0:T(8,128)(2,1)} custom-call(bf16[12,48,3072]{2,1,0:T(8,128)(2,1)S(1)} %get-tuple-element.24.own_ref.refs_0_, bf16[2,2,24,120]{3,2,1,0:T(8,128)(2,1)S(1)} %collective-permute-done.low_ref.refs_3_, bf16[12,2,24,120]{3,2,1,0:T(8,128)(2,1)S(1)} %copy-done.9, ...), custom_call_target="tpu_custom_call" | custom-call | tf_op jit(solution)/shard_map/fold/pallas_call | solution.py:327
  131.9 1.8 copy-done.1
  133.7 1.2 copy-done.5
  134.9 1.2 copy-done.7
  136.1 1.1 copy-done.12
  137.2 1.1 copy-done.14
  138.3 3.8 %spread_out.3 = (bf16[12,32,3072]{2,1,0:T(8,128)(2,1)S(1)}, bf16[2,80,3072]{2,1,0:T(8,128)(2,1)S(1)}, bf16[2,80,3072]{2,1,0:T(8,128)(2,1)S(1)}) custom-call(s32[60]{0:T(128)S(1)} %get-tuple-element.44.source_ref, s32[60]{0:T(128)S(1)} %copy-done.16, s32[60]{0:T(128)S(1)} %reshape.20.mask_ref, bf16[16,40,1152]{2,1,0:T(8,128)(2,1)S(1)} %all-to-all-done.1.in_ref, ...), custom_call_target="tpu_custom_call" | custom-call | tf_op jit(solution)/shard_map/spread_out/pallas_call | solution.py:204
  142.5 4.3 %collective-permute-start.3 = (bf16[2,80,3072]{2,1,0:T(8,128)(2,1)S(1)}, bf16[2,80,3072]{2,1,0:T(8,128)(2,1)S(1)}, u32[]{:S(2)}, u32[]{:S(2)}) collective-permute-start(bf16[2,80,3072]{2,1,0:T(8,128)(2,1)S(1)} %get-tuple-element.37), channel_id=1, source_target_pairs={{1,0},{2,1},{3,2},{4,3},{5,4},{6,5},{7,6},{8,7},{9,8},{10,9},{11,1... | collective-permute-start | bytes 2949128 | tf_op jit(solution)/shard_map/ppermute | solution.py:628
  146.8 32.5 %chi.1 = (f32[12,5,2,4624]{3,2,1,0:T(2,128)}, bf16[6,160,3072]{2,1,0:T(8,128)(2,1)}) custom-call(bf16[12,48,3072]{2,1,0:T(8,128)(2,1)S(1)} %copy-done.2, bf16[12,32,3072]{2,1,0:T(8,128)(2,1)S(1)} %get-tuple-element.33.refs_1_, bf16[14,3,96,3072]{3,2,1,0:T(8,128)(2,1)} %fold.1.refs_2_, bf16[2,2,24,120]{3,2,1,0:T(8,128)(2,1)S(1)} %collective-permute-done.low_ref.refs_3_, ...), custom_call_target="tpu_custom_call" | custom-call | tf_op jit(solution)/shard_map/chi/pallas_call | solution.py:528
  179.4 2.7 %copy-done.3 = bf16[6,160,3072]{2,1,0:T(8,128)(2,1)S(1)} copy-done((bf16[6,160,3072]{2,1,0:T(8,128)(2,1)S(1)}, bf16[6,160,3072]{2,1,0:T(8,128)(2,1)}, u32[]{:S(2)}) %copy-start.3) | copy-done | bytes 5898264
  182.0 3.4 %edge.1 = f32[12,5,2,4624]{3,2,1,0:T(2,128)} custom-call(bf16[6,160,3072]{2,1,0:T(8,128)(2,1)S(1)} %copy-done.3, bf16[2,80,3072]{2,1,0:T(8,128)(2,1)S(1)} %collective-permute-done.2.below_ref, bf16[2,80,3072]{2,1,0:T(8,128)(2,1)S(1)} %collective-permute-done.3.above_ref, f32[12,5,2,4624]{3,2,1,0:T(2,128)} %get-tuple-element.38.chi_ref), custom_call_target="tpu_custom_call", output_to_operand_aliasing={{}: (3, {})} | custom-call | tf_op jit(solution)/shard_map/edge/pallas_call | solution.py:602
  (54 shorter events, 6.1 us)
Async XLA Ops:
  9.6 7.5 %copy-start.17 = (bf16[2,2,12,5,576]{4,1,3,2,0:T(2,128)(2,1)S(1)}, bf16[2,2,12,5,576]{4,1,3,2,0:T(2,128)(2,1)}, u32[]{:S(2)}) copy-start(bf16[2,2,12,5,576]{4,1,3,2,0:T(2,128)(2,1)} %param.17) | copy-start | bytes 829444
  9.6 74.1 %all-to-all-start = ((bf16[16,96,1152]{2,1,0:T(8,128)(2,1)}), bf16[16,96,1152]{2,1,0:T(8,128)(2,1)}, u32[]{:S(2)}, u32[]{:S(2)}) async-start(bf16[16,96,1152]{2,1,0:T(8,128)(2,1)} %pack_blocks.2), calls=%async_computation | async-start | bytes 7077888 | tf_op jit(solution)/shard_map/all_to_all | solution.py:665
  18.6 61.6 %collective-permute-start = (bf16[2,2,24,120]{3,2,1,0:T(8,128)(2,1)S(1)}, bf16[2,2,24,120]{3,2,1,0:T(8,128)(2,1)S(1)}, u32[]{:S(2)}, u32[]{:S(2)}) collective-permute-start(bf16[2,2,24,120]{3,2,1,0:T(8,128)(2,1)S(1)} %slice.34), channel_id=1, source_target_pairs={{0,1},{1,2},{2,3},{3,4},{4,5},{5,6},{6,7},{7,8},{8,9},{9,10},{10,1... | collective-permute-start | bytes 69128 | tf_op jit(solution)/shard_map/ppermute | solution.py:628
  19.2 61.0 %collective-permute-start.1 = (bf16[2,2,24,120]{3,2,1,0:T(8,128)(2,1)S(1)}, bf16[2,2,24,120]{3,2,1,0:T(8,128)(2,1)S(1)}, u32[]{:S(2)}, u32[]{:S(2)}) collective-permute-start(bf16[2,2,24,120]{3,2,1,0:T(8,128)(2,1)S(1)} %slice.36), channel_id=1, source_target_pairs={{1,0},{2,1},{3,2},{4,3},{5,4},{6,5},{7,6},{8,7},{9,8},{10,9},{11,1... | collective-permute-start | bytes 69128 | tf_op jit(solution)/shard_map/ppermute | solution.py:628
  32.0 68.7 %copy-start.18 = (s32[12,5]{0,1:T(8,128)S(1)}, s32[12,5]{0,1:T(8,128)}, u32[]{:S(2)}) copy-start(s32[12,5]{0,1:T(8,128)} %param.18) | copy-start | bytes 724
  32.0 68.9 %copy-start = (bf16[640,768]{1,0:T(8,128)(2,1)S(1)}, bf16[640,768]{1,0:T(8,128)(2,1)}, u32[]{:S(2)}) copy-start(bf16[640,768]{1,0:T(8,128)(2,1)} %constant.36.clone.refs_0_.refs_3_) | copy-start | bytes 2949124
  32.0 68.9 %copy-start.8 = (bf16[640,384]{1,0:T(8,128)(2,1)S(1)}, bf16[640,384]{1,0:T(8,128)(2,1)}, u32[]{:S(2)}) copy-start(bf16[640,384]{1,0:T(8,128)(2,1)} %constant.39.clone.refs_4_) | copy-start | bytes 1474564
  32.0 68.9 %copy-start.16 = (s32[60]{0:T(128)S(1)}, s32[60]{0:T(128)}, u32[]{:S(2)}) copy-start(s32[60]{0:T(128)} %convert_reduce_fusion.rank_ref) | copy-start | bytes 724
  83.7 50.1 %all-to-all-start.1 = ((bf16[16,40,1152]{2,1,0:T(8,128)(2,1)}), bf16[16,40,1152]{2,1,0:T(8,128)(2,1)S(1)}, u32[]{:S(2)}, u32[]{:S(2)}) async-start(bf16[16,40,1152]{2,1,0:T(8,128)(2,1)} %pack_blocks.3), calls=%async_computation.1 | async-start | bytes 2949120 | tf_op jit(solution)/shard_map/all_to_all | solution.py:671
  100.9 1.2 copy-start.4
  102.1 1.2 copy-start.6
  103.3 8.5 %copy-start.9 = (bf16[12,2,24,120]{3,2,1,0:T(8,128)(2,1)S(1)}, bf16[12,2,24,120]{3,2,1,0:T(8,128)(2,1)}, u32[]{:S(2)}) copy-start(bf16[12,2,24,120]{3,2,1,0:T(8,128)(2,1)} %reshape.22.mid_ref.refs_4_) | copy-start | bytes 414724
  103.3 8.5 %copy-start.15 = (bf16[24,192]{1,0:T(8,128)(2,1)S(1)}, bf16[24,192]{1,0:T(8,128)(2,1)}, u32[]{:S(2)}) copy-start(bf16[24,192]{1,0:T(8,128)(2,1)} %constant.35.clone.widen_ref.refs_7_) | copy-start | bytes 27652
  111.0 0.8 copy-start.13
  131.9 1.8 copy-start.1
  133.7 1.2 copy-start.5
  134.9 1.2 copy-start.7
  136.1 1.1 copy-start.12
  137.2 1.1 copy-start.14
  138.3 8.5 %copy-start.2 = (bf16[12,48,3072]{2,1,0:T(8,128)(2,1)S(1)}, bf16[12,48,3072]{2,1,0:T(8,128)(2,1)}, u32[]{:S(2)}) copy-start(bf16[12,48,3072]{2,1,0:T(8,128)(2,1)} %copy-done.1) | copy-start | bytes 10616836
  138.3 8.5 %copy-start.10 = (bf16[12,2,24,120]{3,2,1,0:T(8,128)(2,1)S(1)}, bf16[12,2,24,120]{3,2,1,0:T(8,128)(2,1)}, u32[]{:S(2)}) copy-start(bf16[12,2,24,120]{3,2,1,0:T(8,128)(2,1)} %reshape.22.mid_ref.refs_4_) | copy-start | bytes 414724
  142.1 37.3 %collective-permute-start.2 = (bf16[2,80,3072]{2,1,0:T(8,128)(2,1)S(1)}, bf16[2,80,3072]{2,1,0:T(8,128)(2,1)S(1)}, u32[]{:S(2)}, u32[]{:S(2)}) collective-permute-start(bf16[2,80,3072]{2,1,0:T(8,128)(2,1)S(1)} %get-tuple-element.36), channel_id=1, source_target_pairs={{0,1},{1,2},{2,3},{3,4},{4,5},{5,6},{6,7},{7,8},{8,9},{9,10},{10,1... | collective-permute-start | bytes 2949128 | tf_op jit(solution)/shard_map/ppermute | solution.py:628
  142.5 36.8 %collective-permute-start.3 = (bf16[2,80,3072]{2,1,0:T(8,128)(2,1)S(1)}, bf16[2,80,3072]{2,1,0:T(8,128)(2,1)S(1)}, u32[]{:S(2)}, u32[]{:S(2)}) collective-permute-start(bf16[2,80,3072]{2,1,0:T(8,128)(2,1)S(1)} %get-tuple-element.37), channel_id=1, source_target_pairs={{1,0},{2,1},{3,2},{4,3},{5,4},{6,5},{7,6},{8,7},{9,8},{10,9},{11,1... | collective-permute-start | bytes 2949128 | tf_op jit(solution)/shard_map/ppermute | solution.py:628
  179.4 2.7 %copy-start.3 = (bf16[6,160,3072]{2,1,0:T(8,128)(2,1)S(1)}, bf16[6,160,3072]{2,1,0:T(8,128)(2,1)}, u32[]{:S(2)}) copy-start(bf16[6,160,3072]{2,1,0:T(8,128)(2,1)} %get-tuple-element.35.edge_ref) | copy-start | bytes 17694724
  (1 other events, 0.8 us)

commit v5 on v4

--- a/solution.py
+++ b/solution.py
@@ -18,7 +18,7 @@
 BF = jnp.bfloat16
 F32 = jnp.float32
 MIB = 1024 * 1024
-VMEM = {"pack_blocks": 56, "spread_out": 30, "fold": 44, "chi": 46, "edge": 16}
+VMEM = {"pack_blocks": 56, "spread_out": 30, "fold": 40, "chi": 40, "edge": 16}
 
 
 def call(body, name, grid, in_specs, out_specs, out_shape, scratch=(), prefetch=0):

time: 186 us -> 183 us (0.984)
  local copies, waits for them, and re-layouts: 18.1 us -> 15.5 us
    unnamed x43 -> x41, local copies, waits for them, and re-layouts: 14.4 us -> 11.7 us
  transfers between devices with their start and end apart: 6 -> 6, of which waited for: 2 -> 2; matrix products, arithmetic and copies ran while one was open for 2% -> 2% of each run, Pallas kernels for 35% -> 36%
where the time goes in v5:
time: 183 us
  Pallas kernels  79.9 us (44%)
  waiting for transfers between devices  51.7 us (28%)
  starting transfers between devices  33.8 us (18%)
  local copies, waits for them, and re-layouts  15.5 us (8%)
    ppermute x4, waiting for transfers between devices, ring(): return (lax.ppermute(low, 'row', up), lax.ppermute(high, 'row', down))  48.2 us
    pallas_call x1, Pallas kernels, chi_kernel(): call(body, 'chi', (units + HALF,), [pl.BlockSpec(memory_space=pl.ANY)] *...  32.3 us
    pallas_call x1, Pallas kernels, fold_kernel(): call(body, 'fold', (units,), [pl.BlockSpec((1, *own.shape[1:]), lambda u:...  20.1 us
    all_to_all x1, starting transfers between devices, shards(): lax.all_to_all(sent, 'row', split_axis=0, concat_axis=0, tiled=True)  17 us
    pallas_call x2, Pallas kernels, pack_blocks(): call(body, 'pack_blocks', (steps,), [pl.BlockSpec((batch, 16, size), lamb...  13.5 us
    unnamed x41, local copies, waits for them, and re-layouts  11.7 us
    pallas_call x2, Pallas kernels, spread_out(): call(body, 'spread_out', (steps,), [pl.BlockSpec(incoming.shape, lambda a...  10.6 us
    ppermute x4, starting transfers between devices, ring(): return (lax.ppermute(low, 'row', up), lax.ppermute(high, 'row', down))  9.31 us
  transfers between devices with their start and end apart: 6, of which 2 were waited for; matrix products, arithmetic and copies ran while one was open for 2% of the time, Pallas kernels for 36%

profile of v5, /device:TPU:0, one launch (start us, length us, event | category | flops | bytes accessed | tf_op | source)
XLA Modules:
  0.0 182.7 jit_solution(7294999976856274201)
XLA Ops:
  0.9 0.8 convert_reduce_fusion.rank_ref
  2.1 7.4 %pack_blocks.2 = bf16[16,96,1152]{2,1,0:T(8,128)(2,1)} custom-call(s32[60]{0:T(128)} %get-tuple-element.43.target_ref, s32[60]{0:T(128)} %convert_reduce_fusion.rank_ref, bf16[60,68,576]{2,1,0:T(8,128)(2,1)} %bitcast.14, bf16[60,68,576]{2,1,0:T(8,128)(2,1)} %bitcast.15, bf16[60,68,576]{2,1,0:T(8,128)(2,1)} %bitcast.16), custom_call_target="tpu_custom_call" | custom-call | tf_op jit(solution)/shard_map/pack_blocks/pallas_call | solution.py:87
  9.6 7.5 %all-to-all-start = ((bf16[16,96,1152]{2,1,0:T(8,128)(2,1)}), bf16[16,96,1152]{2,1,0:T(8,128)(2,1)}, u32[]{:S(2)}, u32[]{:S(2)}) async-start(bf16[16,96,1152]{2,1,0:T(8,128)(2,1)} %pack_blocks.2), calls=%async_computation | async-start | bytes 7077888 | tf_op jit(solution)/shard_map/all_to_all | solution.py:665
  19.1 4.1 %collective-permute-start.1 = (bf16[2,2,24,120]{3,2,1,0:T(8,128)(2,1)S(1)}, bf16[2,2,24,120]{3,2,1,0:T(8,128)(2,1)S(1)}, u32[]{:S(2)}, u32[]{:S(2)}) collective-permute-start(bf16[2,2,24,120]{3,2,1,0:T(8,128)(2,1)S(1)} %slice.36), channel_id=1, source_target_pairs={{1,0},{2,1},{3,2},{4,3},{5,4},{6,5},{7,6},{8,7},{9,8},{10,9},{11,1... | collective-permute-start | bytes 69128 | tf_op jit(solution)/shard_map/ppermute | solution.py:628
  24.6 1.2 reshape.22.mid_ref.refs_4_
  25.8 6.1 %pack_blocks.3 = bf16[16,40,1152]{2,1,0:T(8,128)(2,1)} custom-call(s32[60]{0:T(128)} %get-tuple-element.43.target_ref, s32[60]{0:T(128)} %convert_reduce_fusion.rank_ref, bf16[60,68,576]{2,1,0:T(8,128)(2,1)} %bitcast.17, bf16[60,68,576]{2,1,0:T(8,128)(2,1)} %bitcast.18), custom_call_target="tpu_custom_call" | custom-call | tf_op jit(solution)/shard_map/pack_blocks/pallas_call | solution.py:87
  31.9 48.2 %collective-permute-done.low_ref.refs_3_ = bf16[2,2,24,120]{3,2,1,0:T(8,128)(2,1)S(1)} collective-permute-done((bf16[2,2,24,120]{3,2,1,0:T(8,128)(2,1)S(1)}, bf16[2,2,24,120]{3,2,1,0:T(8,128)(2,1)S(1)}, u32[]{:S(2)}, u32[]{:S(2)}) %collective-permute-start) | collective-permute-done | bytes 23072 | tf_op jit(solution)/shard_map/ppermute | solution.py:628
  80.1 3.5 %all-to-all-done.in_ref = bf16[16,96,1152]{2,1,0:T(8,128)(2,1)} async-done(((bf16[16,96,1152]{2,1,0:T(8,128)(2,1)}), bf16[16,96,1152]{2,1,0:T(8,128)(2,1)}, u32[]{:S(2)}, u32[]{:S(2)}) %all-to-all-start) | async-done | bytes 3538976 | tf_op jit(solution)/shard_map/all_to_all | solution.py:665
  83.6 17.0 %all-to-all-start.1 = ((bf16[16,40,1152]{2,1,0:T(8,128)(2,1)}), bf16[16,40,1152]{2,1,0:T(8,128)(2,1)S(1)}, u32[]{:S(2)}, u32[]{:S(2)}) async-start(bf16[16,40,1152]{2,1,0:T(8,128)(2,1)} %pack_blocks.3), calls=%async_computation.1 | async-start | bytes 2949120 | tf_op jit(solution)/shard_map/all_to_all | solution.py:671
  100.9 1.2 copy-done.3
  102.1 1.2 copy-done.5
  103.3 6.8 %spread_out.2 = (bf16[12,48,3072]{2,1,0:T(8,128)(2,1)S(1)}, bf16[2,48,3072]{2,1,0:T(8,128)(2,1)S(1)}, bf16[2,48,3072]{2,1,0:T(8,128)(2,1)S(1)}) custom-call(s32[60]{0:T(128)S(1)} %get-tuple-element.44.source_ref, s32[60]{0:T(128)S(1)} %copy-done.15, s32[60]{0:T(128)S(1)} %reshape.20.mask_ref, bf16[16,96,1152]{2,1,0:T(8,128)(2,1)} %all-to-all-done.in_ref, ...), custom_call_target="tpu_custom_call" | custom-call | tf_op jit(solution)/shard_map/spread_out/pallas_call | solution.py:204
  110.1 0.8 copy-done.10
  110.9 0.9 copy-done.12
  111.8 20.1 %fold.1.refs_2_ = bf16[14,3,96,3072]{3,2,1,0:T(8,128)(2,1)} custom-call(bf16[12,48,3072]{2,1,0:T(8,128)(2,1)S(1)} %get-tuple-element.24.own_ref.refs_0_, bf16[2,2,24,120]{3,2,1,0:T(8,128)(2,1)S(1)} %collective-permute-done.low_ref.refs_3_, bf16[12,2,24,120]{3,2,1,0:T(8,128)(2,1)S(1)} %copy-done.8, ...), custom_call_target="tpu_custom_call" | custom-call | tf_op jit(solution)/shard_map/fold/pallas_call | solution.py:327
  131.9 1.8 copy-done.1
  133.7 1.2 copy-done.4
  134.9 1.2 copy-done.6
  136.1 1.1 copy-done.11
  137.1 1.1 copy-done.13
  138.2 3.8 %spread_out.3 = (bf16[12,32,3072]{2,1,0:T(8,128)(2,1)S(1)}, bf16[2,80,3072]{2,1,0:T(8,128)(2,1)S(1)}, bf16[2,80,3072]{2,1,0:T(8,128)(2,1)S(1)}) custom-call(s32[60]{0:T(128)S(1)} %get-tuple-element.44.source_ref, s32[60]{0:T(128)S(1)} %copy-done.15, s32[60]{0:T(128)S(1)} %reshape.20.mask_ref, bf16[16,40,1152]{2,1,0:T(8,128)(2,1)S(1)} %all-to-all-done.1.in_ref, ...), custom_call_target="tpu_custom_call" | custom-call | tf_op jit(solution)/shard_map/spread_out/pallas_call | solution.py:204
  142.5 4.3 %collective-permute-start.3 = (bf16[2,80,3072]{2,1,0:T(8,128)(2,1)S(1)}, bf16[2,80,3072]{2,1,0:T(8,128)(2,1)S(1)}, u32[]{:S(2)}, u32[]{:S(2)}) collective-permute-start(bf16[2,80,3072]{2,1,0:T(8,128)(2,1)S(1)} %get-tuple-element.37), channel_id=1, source_target_pairs={{1,0},{2,1},{3,2},{4,3},{5,4},{6,5},{7,6},{8,7},{9,8},{10,9},{11,1... | collective-permute-start | bytes 2949128 | tf_op jit(solution)/shard_map/ppermute | solution.py:628
  146.8 32.3 %chi.1 = (f32[12,5,2,4624]{3,2,1,0:T(2,128)}, bf16[6,160,3072]{2,1,0:T(8,128)(2,1)S(1)}) custom-call(bf16[12,48,3072]{2,1,0:T(8,128)(2,1)S(1)} %copy-done.2, bf16[12,32,3072]{2,1,0:T(8,128)(2,1)S(1)} %get-tuple-element.33.refs_1_, bf16[14,3,96,3072]{3,2,1,0:T(8,128)(2,1)} %fold.1.refs_2_, bf16[2,2,24,120]{3,2,1,0:T(8,128)(2,1)S(1)} %collective-permute-done.low_ref.refs_3_, ...), custom_call_target="tpu_custom_call" | custom-call | tf_op jit(solution)/shard_map/chi/pallas_call | solution.py:528
  179.1 3.4 %edge.1 = f32[12,5,2,4624]{3,2,1,0:T(2,128)} custom-call(bf16[6,160,3072]{2,1,0:T(8,128)(2,1)S(1)} %get-tuple-element.35.edge_ref, bf16[2,80,3072]{2,1,0:T(8,128)(2,1)S(1)} %collective-permute-done.2.below_ref, bf16[2,80,3072]{2,1,0:T(8,128)(2,1)S(1)} %collective-permute-done.3.above_ref, ...), custom_call_target="tpu_custom_call", output_to_operand_aliasing={{}: (3, {})} | custom-call | tf_op jit(solution)/shard_map/edge/pallas_call | solution.py:602
  (52 shorter events, 5.4 us)
Async XLA Ops:
  9.5 7.5 %copy-start.16 = (bf16[2,2,12,5,576]{4,1,3,2,0:T(2,128)(2,1)S(1)}, bf16[2,2,12,5,576]{4,1,3,2,0:T(2,128)(2,1)}, u32[]{:S(2)}) copy-start(bf16[2,2,12,5,576]{4,1,3,2,0:T(2,128)(2,1)} %param.17) | copy-start | bytes 829444
  9.6 74.1 %all-to-all-start = ((bf16[16,96,1152]{2,1,0:T(8,128)(2,1)}), bf16[16,96,1152]{2,1,0:T(8,128)(2,1)}, u32[]{:S(2)}, u32[]{:S(2)}) async-start(bf16[16,96,1152]{2,1,0:T(8,128)(2,1)} %pack_blocks.2), calls=%async_computation | async-start | bytes 7077888 | tf_op jit(solution)/shard_map/all_to_all | solution.py:665
  18.6 61.6 %collective-permute-start = (bf16[2,2,24,120]{3,2,1,0:T(8,128)(2,1)S(1)}, bf16[2,2,24,120]{3,2,1,0:T(8,128)(2,1)S(1)}, u32[]{:S(2)}, u32[]{:S(2)}) collective-permute-start(bf16[2,2,24,120]{3,2,1,0:T(8,128)(2,1)S(1)} %slice.34), channel_id=1, source_target_pairs={{0,1},{1,2},{2,3},{3,4},{4,5},{5,6},{6,7},{7,8},{8,9},{9,10},{10,1... | collective-permute-start | bytes 69128 | tf_op jit(solution)/shard_map/ppermute | solution.py:628
  19.1 61.0 %collective-permute-start.1 = (bf16[2,2,24,120]{3,2,1,0:T(8,128)(2,1)S(1)}, bf16[2,2,24,120]{3,2,1,0:T(8,128)(2,1)S(1)}, u32[]{:S(2)}, u32[]{:S(2)}) collective-permute-start(bf16[2,2,24,120]{3,2,1,0:T(8,128)(2,1)S(1)} %slice.36), channel_id=1, source_target_pairs={{1,0},{2,1},{3,2},{4,3},{5,4},{6,5},{7,6},{8,7},{9,8},{10,9},{11,1... | collective-permute-start | bytes 69128 | tf_op jit(solution)/shard_map/ppermute | solution.py:628
  31.9 68.7 %copy-start.17 = (s32[12,5]{0,1:T(8,128)S(1)}, s32[12,5]{0,1:T(8,128)}, u32[]{:S(2)}) copy-start(s32[12,5]{0,1:T(8,128)} %param.18) | copy-start | bytes 724
  31.9 68.9 %copy-start = (bf16[640,768]{1,0:T(8,128)(2,1)S(1)}, bf16[640,768]{1,0:T(8,128)(2,1)}, u32[]{:S(2)}) copy-start(bf16[640,768]{1,0:T(8,128)(2,1)} %constant.36.clone.refs_0_.refs_3_) | copy-start | bytes 2949124
  31.9 68.9 %copy-start.7 = (bf16[640,384]{1,0:T(8,128)(2,1)S(1)}, bf16[640,384]{1,0:T(8,128)(2,1)}, u32[]{:S(2)}) copy-start(bf16[640,384]{1,0:T(8,128)(2,1)} %constant.39.clone.refs_4_) | copy-start | bytes 1474564
  31.9 68.9 %copy-start.15 = (s32[60]{0:T(128)S(1)}, s32[60]{0:T(128)}, u32[]{:S(2)}) copy-start(s32[60]{0:T(128)} %convert_reduce_fusion.rank_ref) | copy-start | bytes 724
  83.6 50.0 %all-to-all-start.1 = ((bf16[16,40,1152]{2,1,0:T(8,128)(2,1)}), bf16[16,40,1152]{2,1,0:T(8,128)(2,1)S(1)}, u32[]{:S(2)}, u32[]{:S(2)}) async-start(bf16[16,40,1152]{2,1,0:T(8,128)(2,1)} %pack_blocks.3), calls=%async_computation.1 | async-start | bytes 2949120 | tf_op jit(solution)/shard_map/all_to_all | solution.py:671
  100.9 1.2 copy-start.3
  102.1 1.2 copy-start.5
  103.3 8.5 %copy-start.8 = (bf16[12,2,24,120]{3,2,1,0:T(8,128)(2,1)S(1)}, bf16[12,2,24,120]{3,2,1,0:T(8,128)(2,1)}, u32[]{:S(2)}) copy-start(bf16[12,2,24,120]{3,2,1,0:T(8,128)(2,1)} %reshape.22.mid_ref.refs_4_) | copy-start | bytes 414724
  103.3 8.5 %copy-start.14 = (bf16[24,192]{1,0:T(8,128)(2,1)S(1)}, bf16[24,192]{1,0:T(8,128)(2,1)}, u32[]{:S(2)}) copy-start(bf16[24,192]{1,0:T(8,128)(2,1)} %constant.35.clone.widen_ref.refs_7_) | copy-start | bytes 27652
  110.1 0.8 copy-start.10
  110.9 0.9 copy-start.12
  131.9 1.8 copy-start.1
  133.7 1.2 copy-start.4
  134.9 1.2 copy-start.6
  136.1 1.1 copy-start.11
  137.1 1.1 copy-start.13
  138.2 8.6 %copy-start.2 = (bf16[12,48,3072]{2,1,0:T(8,128)(2,1)S(1)}, bf16[12,48,3072]{2,1,0:T(8,128)(2,1)}, u32[]{:S(2)}) copy-start(bf16[12,48,3072]{2,1,0:T(8,128)(2,1)} %copy-done.1) | copy-start | bytes 10616836
  138.2 8.6 %copy-start.9 = (bf16[12,2,24,120]{3,2,1,0:T(8,128)(2,1)S(1)}, bf16[12,2,24,120]{3,2,1,0:T(8,128)(2,1)}, u32[]{:S(2)}) copy-start(bf16[12,2,24,120]{3,2,1,0:T(8,128)(2,1)} %reshape.22.mid_ref.refs_4_) | copy-start | bytes 414724
  142.0 37.1 %collective-permute-start.2 = (bf16[2,80,3072]{2,1,0:T(8,128)(2,1)S(1)}, bf16[2,80,3072]{2,1,0:T(8,128)(2,1)S(1)}, u32[]{:S(2)}, u32[]{:S(2)}) collective-permute-start(bf16[2,80,3072]{2,1,0:T(8,128)(2,1)S(1)} %get-tuple-element.36), channel_id=1, source_target_pairs={{0,1},{1,2},{2,3},{3,4},{4,5},{5,6},{6,7},{7,8},{8,9},{9,10},{10,1... | collective-permute-start | bytes 2949128 | tf_op jit(solution)/shard_map/ppermute | solution.py:628
  142.5 36.6 %collective-permute-start.3 = (bf16[2,80,3072]{2,1,0:T(8,128)(2,1)S(1)}, bf16[2,80,3072]{2,1,0:T(8,128)(2,1)S(1)}, u32[]{:S(2)}, u32[]{:S(2)}) collective-permute-start(bf16[2,80,3072]{2,1,0:T(8,128)(2,1)S(1)} %get-tuple-element.37), channel_id=1, source_target_pairs={{1,0},{2,1},{3,2},{4,3},{5,4},{6,5},{7,6},{8,7},{9,8},{10,9},{11,1... | collective-permute-start | bytes 2949128 | tf_op jit(solution)/shard_map/ppermute | solution.py:628
